TPU v7x, 32 devices: a whole 2x2x4 slice. The times are simulated.
32 devices in a mesh: seq: 4 (over y, x), dp: 8 (over z, core).
Axes of the slice: x: 2, y: 2, z: 4, core: 2. Of those that a mesh axis runs over, the one named last changes fastest.
Arguments:
- hidden: bfloat16 [3, 16, 256, 1024], P(None, 'dp', 'seq'), may hold values from -6 to 6
- encoder: bfloat16 [16, 256, 1024], P('dp', 'seq'), may hold values from -6 to 6
- lengths: int32 [16], P('dp'), may hold values from 1 to 256, as said below
- enc_lengths: int32 [16], P('dp'), may hold values from 1 to 256, as said below
- w_query: bfloat16 [1024, 1024], P('dp'), may hold values from -0.1875 to 0.1875
- w_key: bfloat16 [1024, 1024], P('dp'), may hold values from -0.1875 to 0.1875
- w_value: bfloat16 [1024, 1024], P('dp'), may hold values from -0.1875 to 0.1875
- w_attn_out: bfloat16 [1024, 1024], P('dp'), may hold values from -0.75 to 0.75
- w_relative: bfloat16 [1024, 512], P('dp'), may hold values from -0.1875 to 0.1875
- w_cross_query: bfloat16 [1024, 1024], P('dp'), may hold values from -0.1875 to 0.1875
- w_cross_key: bfloat16 [1024, 1024], P('dp'), may hold values from -0.1875 to 0.1875
- w_cross_value: bfloat16 [1024, 1024], P('dp'), may hold values from -0.1875 to 0.1875
- w_cross_out: bfloat16 [1024, 1024], P('dp'), may hold values from -0.75 to 0.75
- w_up: bfloat16 [1024, 4096], P('dp'), may hold values from -0.1875 to 0.1875
- w_down: bfloat16 [4096, 1024], P('dp'), may hold values from -0.09375 to 0.09375
- gain_attn: bfloat16 [1024], P('dp'), may hold values from 0.099609375 to 1.8984375
- gain_cross: bfloat16 [1024], P('dp'), may hold values from 0.099609375 to 1.8984375
- gain_ffn: bfloat16 [1024], P('dp'), may hold values from 0.099609375 to 1.8984375
- cotangent: bfloat16 [3, 16, 256, 1024], P(None, 'dp', 'seq'), may hold values from -6 to 6
Outputs:
- output: bfloat16 [3, 16, 256, 1024], P(None, 'dp', 'seq')
- hidden_grad: float32 [3, 16, 256, 1024], P(None, 'dp', 'seq')
- encoder_grad: float32 [16, 256, 1024], P('dp', 'seq')
- query_grad: float32 [1024, 1024], P(('seq', 'dp'))
- key_grad: float32 [1024, 1024], P(('seq', 'dp'))
- value_grad: float32 [1024, 1024], P(('seq', 'dp'))
- attn_out_grad: float32 [1024, 1024], P(('seq', 'dp'))
- relative_grad: float32 [1024, 512], P(('seq', 'dp'))
- cross_query_grad: float32 [1024, 1024], P(('seq', 'dp'))
- cross_key_grad: float32 [1024, 1024], P(('seq', 'dp'))
- cross_value_grad: float32 [1024, 1024], P(('seq', 'dp'))
- cross_out_grad: float32 [1024, 1024], P(('seq', 'dp'))
- up_grad: float32 [1024, 4096], P(('seq', 'dp'))
- down_grad: float32 [4096, 1024], P(('seq', 'dp'))
- gain_attn_grad: float32 [1024], P(('seq', 'dp'))
- gain_cross_grad: float32 [1024], P(('seq', 'dp'))
- gain_ffn_grad: float32 [1024], P(('seq', 'dp'))
Inputs may be any that keep to these rules, and one draw needn't show every extreme that they name: `lengths`: among the 2 rows of each index of dp, one has length 256. `enc_lengths`: among the 2 rows of each index of dp, one has encoder length 256.
All inputs are finite; a program needn't handle non-finite values.
Results may differ from a plain program's by a relative error of at most 0.02.
Values may be sent and summed in bfloat16 or wider, within the bound.
A program may use at most 320 MiB of HBM per device.

v0:
```python
import math

import jax
import jax.numpy as jnp
from jax import lax
from jax.sharding import PartitionSpec as P

HEADS = 16
HEAD_DIM = 64
BUCKETS = 32


eps_norm = 1e-05
bucket_edges = [step_index for step_index in range(1, 16)] + [
    int(math.ceil(16 * 8 ** ((step_index - 16) / 16))) for step_index in range(16, 32)
]


def layer_norm(values, gain_vec):
    row_mean = jnp.mean(values, axis=-1, keepdims=True)
    centred = values - row_mean
    row_var = jnp.mean(centred * centred, axis=-1, keepdims=True)
    return centred * lax.rsqrt(row_var + eps_norm) * gain_vec


def bucket_hot(query_pos, key_pos, hot_type):
    distance = jnp.maximum(query_pos[:, None] - key_pos[None, :], 0)
    edges = jnp.array(bucket_edges, jnp.int32)
    bucket = jnp.sum((distance[:, :, None] >= edges[None, None, :]).astype(jnp.int32), axis=2)
    return (bucket[:, :, None] == jnp.arange(BUCKETS, dtype=jnp.int32)[None, None, :]).astype(
        hot_type
    )


def score_masks(query_pos, key_pos, row_lengths, streams):
    stream_index = jnp.arange(streams)[:, None, None, None, None]
    main_mask = key_pos[None, :] <= query_pos[:, None]
    ahead_mask = key_pos[None, :] < query_pos[:, None]
    causal = jnp.where(stream_index == 0, main_mask[None, None, None], ahead_mask[None, None, None])
    live_keys = (key_pos[None, :] < row_lengths[:, None])[None, :, None, None, :]
    own_ok = jnp.arange(streams)[:, None, None, None] > 0
    return (causal & live_keys, own_ok)


def stream_softmax(main_scores, own_scores):
    peak_score = jnp.maximum(jnp.max(main_scores, axis=-1), own_scores)
    main_exp = jnp.exp(main_scores - peak_score[..., None])
    own_exp = jnp.exp(own_scores - peak_score)
    denominator = jnp.sum(main_exp, axis=-1) + own_exp
    return (main_exp / denominator[..., None], own_exp / denominator)


def cross_softmax(scores):
    peak_score = jnp.max(scores, axis=-1, keepdims=True)
    exps = jnp.exp(scores - peak_score)
    return exps / jnp.sum(exps, axis=-1, keepdims=True)


def exact_gelu(values):
    return jax.nn.gelu(values, approximate=False)


def flatten_rows(array):
    return array.reshape(-1, array.shape[-1])


def project(array, weight):
    result = jnp.dot(flatten_rows(array), weight, preferred_element_type=jnp.float32)
    return result.reshape(array.shape[:-1] + (weight.shape[1],))


def project_back(grad_rows, weight):
    result = jnp.einsum(
        "ne,de->nd", flatten_rows(grad_rows), weight, preferred_element_type=jnp.float32
    )
    return result.reshape(grad_rows.shape[:-1] + (weight.shape[0],))


def weight_grad(array, grad_rows):
    return jnp.einsum(
        "nd,ne->de",
        flatten_rows(array),
        flatten_rows(grad_rows),
        preferred_element_type=jnp.float32,
    )


def turned(array):
    return jnp.transpose(array, (0, 1, 3, 2))


def local(
    hidden,
    encoder,
    lengths,
    enc_lengths,
    w_query,
    w_key,
    w_value,
    w_attn_out,
    w_relative,
    w_cross_query,
    w_cross_key,
    w_cross_value,
    w_cross_out,
    w_up,
    w_down,
    gain_attn,
    gain_cross,
    gain_ffn,
    cotangent,
):
    (
        full_query,
        full_key,
        full_value,
        full_attn_out,
        full_relative,
        full_cquery,
        full_ckey,
        full_cvalue,
        full_cout,
        full_up,
        full_down,
        full_gain_attn,
        full_gain_cross,
        full_gain_ffn,
    ) = (
        lax.all_gather(w_query, "dp", axis=0, tiled=True),
        lax.all_gather(w_key, "dp", axis=0, tiled=True),
        lax.all_gather(w_value, "dp", axis=0, tiled=True),
        lax.all_gather(w_attn_out, "dp", axis=0, tiled=True),
        lax.all_gather(w_relative, "dp", axis=0, tiled=True),
        lax.all_gather(w_cross_query, "dp", axis=0, tiled=True),
        lax.all_gather(w_cross_key, "dp", axis=0, tiled=True),
        lax.all_gather(w_cross_value, "dp", axis=0, tiled=True),
        lax.all_gather(w_cross_out, "dp", axis=0, tiled=True),
        lax.all_gather(w_up, "dp", axis=0, tiled=True),
        lax.all_gather(w_down, "dp", axis=0, tiled=True),
        lax.all_gather(gain_attn, "dp", axis=0, tiled=True),
        lax.all_gather(gain_cross, "dp", axis=0, tiled=True),
        lax.all_gather(gain_ffn, "dp", axis=0, tiled=True),
    )
    streams, row_count, local_len, width = hidden.shape
    enc_local = encoder.shape[1]
    seq_len = local_len * lax.axis_size("seq")
    enc_len = enc_local * lax.axis_size("seq")
    head_shape = (streams, row_count, local_len, HEADS, HEAD_DIM)
    flat_shape = (streams, row_count, local_len, width)
    query_low = (project(hidden, full_query) * 0.125).astype(jnp.bfloat16)
    key_low = project(hidden, full_key).astype(jnp.bfloat16)
    value_low = project(hidden, full_value).astype(jnp.bfloat16)
    rel_low = project(hidden, full_relative).astype(jnp.bfloat16)
    enc_key_low = project(encoder, full_ckey).astype(jnp.bfloat16)
    enc_value_low = project(encoder, full_cvalue).astype(jnp.bfloat16)
    main_keys, main_values, enc_keys, enc_values = (
        lax.all_gather(key_low[0], "seq", axis=1, tiled=True),
        lax.all_gather(value_low[0], "seq", axis=1, tiled=True),
        lax.all_gather(enc_key_low, "seq", axis=1, tiled=True),
        lax.all_gather(enc_value_low, "seq", axis=1, tiled=True),
    )
    query_heads = query_low.reshape(head_shape)
    key_heads = key_low.reshape(head_shape)
    value_heads = value_low.reshape(head_shape)
    rel_heads = rel_low.reshape(streams, row_count, local_len, HEADS, BUCKETS)
    all_keys = main_keys.reshape(row_count, seq_len, HEADS, HEAD_DIM)
    all_values = main_values.reshape(row_count, seq_len, HEADS, HEAD_DIM)
    all_enc_keys = enc_keys.reshape(row_count, enc_len, HEADS, HEAD_DIM)
    all_enc_values = enc_values.reshape(row_count, enc_len, HEADS, HEAD_DIM)
    query_pos = lax.axis_index("seq") * local_len + jnp.arange(local_len, dtype=jnp.int32)
    key_pos = jnp.arange(seq_len, dtype=jnp.int32)
    hot = bucket_hot(query_pos, key_pos, jnp.bfloat16)
    allowed, own_ok = score_masks(query_pos, key_pos, lengths, streams)
    raw_scores = jnp.einsum(
        "jrthe,rshe->jrhts", query_heads, all_keys, preferred_element_type=jnp.float32
    )
    rel_bias = jnp.einsum("jrthb,tsb->jrhts", rel_heads, hot, preferred_element_type=jnp.float32)
    main_scores = jnp.where(allowed, raw_scores + rel_bias, -1000000000.0)
    own_raw = jnp.einsum(
        "jrthe,jrthe->jrth", query_heads, key_heads, preferred_element_type=jnp.float32
    ) + rel_heads[..., 0].astype(jnp.float32)
    own_scores = jnp.where(own_ok, turned(own_raw), -1000000000.0)
    (main_prob, own_prob), softmax_pull = jax.vjp(stream_softmax, main_scores, own_scores)
    main_low = main_prob.astype(jnp.bfloat16)
    context = jnp.einsum(
        "jrhts,rshe->jrthe", main_low, all_values, preferred_element_type=jnp.float32
    )
    context = context + turned(own_prob)[..., None] * value_heads.astype(jnp.float32)
    context_low = context.reshape(flat_shape).astype(jnp.bfloat16)
    attn_out = project(context_low, full_attn_out)
    normed, norm_attn_pull = jax.vjp(
        layer_norm, hidden.astype(jnp.float32) + attn_out, full_gain_attn.astype(jnp.float32)
    )
    normed_low = normed.astype(jnp.bfloat16)
    cross_query_low = (project(normed_low, full_cquery) * 0.125).astype(jnp.bfloat16)
    cross_heads = cross_query_low.reshape(head_shape)
    enc_live = (jnp.arange(enc_len, dtype=jnp.int32)[None, :] < enc_lengths[:, None])[
        None, :, None, None, :
    ]
    cross_raw = jnp.einsum(
        "jrthe,rshe->jrhts", cross_heads, all_enc_keys, preferred_element_type=jnp.float32
    )
    cross_scores = jnp.where(enc_live, cross_raw, -1000000000.0)
    cross_prob, cross_pull = jax.vjp(cross_softmax, cross_scores)
    cross_low = cross_prob.astype(jnp.bfloat16)
    cross_context = jnp.einsum(
        "jrhts,rshe->jrthe", cross_low, all_enc_values, preferred_element_type=jnp.float32
    )
    cross_context_low = cross_context.reshape(flat_shape).astype(jnp.bfloat16)
    cross_out = project(cross_context_low, full_cout)
    crossed, norm_cross_pull = jax.vjp(
        layer_norm, normed + cross_out, full_gain_cross.astype(jnp.float32)
    )
    crossed_low = crossed.astype(jnp.bfloat16)
    upward = project(crossed_low, full_up)
    activated, gelu_pull = jax.vjp(exact_gelu, upward)
    activated_low = activated.astype(jnp.bfloat16)
    down = project(activated_low, full_down)
    result, norm_ffn_pull = jax.vjp(layer_norm, crossed + down, full_gain_ffn.astype(jnp.float32))
    ffn_grad, gainffn_part = norm_ffn_pull(cotangent.astype(jnp.float32))
    down_low = ffn_grad.astype(jnp.bfloat16)
    down_part = weight_grad(activated_low, down_low)
    (upward_grad,) = gelu_pull(project_back(down_low, full_down))
    upward_low = upward_grad.astype(jnp.bfloat16)
    up_part = weight_grad(crossed_low, upward_low)
    crossed_grad = ffn_grad + project_back(upward_low, full_up)
    cross_res_grad, gaincross_part = norm_cross_pull(crossed_grad)
    cross_res_low = cross_res_grad.astype(jnp.bfloat16)
    crossout_part = weight_grad(cross_context_low, cross_res_low)
    cross_ctx_grad = project_back(cross_res_low, full_cout).astype(jnp.bfloat16).reshape(head_shape)
    cross_prob_grad = jnp.einsum(
        "jrthe,rshe->jrhts", cross_ctx_grad, all_enc_values, preferred_element_type=jnp.float32
    )
    enc_value_main = jnp.einsum(
        "jrhts,jrthe->rshe", cross_low, cross_ctx_grad, preferred_element_type=jnp.float32
    )
    (cross_score_grad,) = cross_pull(cross_prob_grad)
    cross_score_low = jnp.where(enc_live, cross_score_grad, 0.0).astype(jnp.bfloat16)
    cross_query_grad = jnp.einsum(
        "jrhts,rshe->jrthe", cross_score_low, all_enc_keys, preferred_element_type=jnp.float32
    )
    enc_key_main = jnp.einsum(
        "jrhts,jrthe->rshe", cross_score_low, cross_heads, preferred_element_type=jnp.float32
    )
    cross_query_back = (cross_query_grad.astype(jnp.bfloat16) * 0.125).reshape(flat_shape)
    normed_grad = cross_res_grad + project_back(cross_query_back, full_cquery)
    crossquery_part = weight_grad(normed_low, cross_query_back)
    residual_grad, gainattn_part = norm_attn_pull(normed_grad)
    attn_low = residual_grad.astype(jnp.bfloat16)
    outproj_part = weight_grad(context_low, attn_low)
    context_grad = project_back(attn_low, full_attn_out).astype(jnp.bfloat16).reshape(head_shape)
    main_prob_grad = jnp.einsum(
        "jrthe,rshe->jrhts", context_grad, all_values, preferred_element_type=jnp.float32
    )
    own_prob_grad = turned(
        jnp.einsum(
            "jrthe,jrthe->jrth", context_grad, value_heads, preferred_element_type=jnp.float32
        )
    )
    value_main = jnp.einsum(
        "jrhts,jrthe->rshe", main_low, context_grad, preferred_element_type=jnp.float32
    )
    value_own = turned(own_prob)[..., None] * context_grad.astype(jnp.float32)
    main_score_grad, own_score_grad = softmax_pull((main_prob_grad, own_prob_grad))
    score_low = jnp.where(allowed, main_score_grad, 0.0).astype(jnp.bfloat16)
    own_grad = turned(jnp.where(own_ok, own_score_grad, 0.0))
    query_grad = jnp.einsum(
        "jrhts,rshe->jrthe", score_low, all_keys, preferred_element_type=jnp.float32
    )
    query_grad = query_grad + own_grad[..., None] * key_heads.astype(jnp.float32)
    key_main = jnp.einsum(
        "jrhts,jrthe->rshe", score_low, query_heads, preferred_element_type=jnp.float32
    )
    key_own = own_grad[..., None] * query_heads.astype(jnp.float32)
    first_bucket = (jnp.arange(BUCKETS) == 0).astype(jnp.float32)
    rel_grad = (
        jnp.einsum("jrhts,tsb->jrthb", score_low, hot, preferred_element_type=jnp.float32)
        + own_grad[..., None] * first_bucket
    )
    key_sum, value_sum, enc_key_sum, enc_value_sum = (
        lax.psum_scatter(
            key_main.astype(jnp.bfloat16), "seq", scatter_dimension=1, tiled=True
        ).astype(jnp.float32),
        lax.psum_scatter(
            value_main.astype(jnp.bfloat16), "seq", scatter_dimension=1, tiled=True
        ).astype(jnp.float32),
        lax.psum_scatter(
            enc_key_main.astype(jnp.bfloat16), "seq", scatter_dimension=1, tiled=True
        ).astype(jnp.float32),
        lax.psum_scatter(
            enc_value_main.astype(jnp.bfloat16), "seq", scatter_dimension=1, tiled=True
        ).astype(jnp.float32),
    )
    key_grad = jnp.concatenate([key_sum[None], key_own[1:]], axis=0)
    value_grad = jnp.concatenate([value_sum[None], value_own[1:]], axis=0)
    query_back = (query_grad.astype(jnp.bfloat16) * 0.125).reshape(flat_shape)
    key_back = key_grad.reshape(flat_shape).astype(jnp.bfloat16)
    value_back = value_grad.reshape(flat_shape).astype(jnp.bfloat16)
    rel_back = rel_grad.reshape(streams, row_count, local_len, HEADS * BUCKETS).astype(jnp.bfloat16)
    enc_key_back = enc_key_sum.reshape(row_count, enc_local, width).astype(jnp.bfloat16)
    enc_value_back = enc_value_sum.reshape(row_count, enc_local, width).astype(jnp.bfloat16)
    encoder_grad = project_back(enc_key_back, full_ckey) + project_back(enc_value_back, full_cvalue)
    hidden_grad = (
        residual_grad + project_back(query_back, full_query) + project_back(key_back, full_key)
    )
    hidden_grad = (
        hidden_grad + project_back(value_back, full_value) + project_back(rel_back, full_relative)
    )
    query_part = weight_grad(hidden, query_back)
    key_part = weight_grad(hidden, key_back)
    value_part = weight_grad(hidden, value_back)
    relative_part = weight_grad(hidden, rel_back)
    crosskey_part = weight_grad(encoder, enc_key_back)
    crossvalue_part = weight_grad(encoder, enc_value_back)
    (
        query_sum,
        keyw_sum,
        valuew_sum,
        outproj_sum,
        relative_sum,
        cquery_sum,
        ckey_sum,
        cvalue_sum,
        cout_sum,
        up_sum,
        down_sum,
        gainattn_sum,
        gaincross_sum,
        gainffn_sum,
    ) = (
        lax.psum_scatter(query_part, ("seq", "dp"), scatter_dimension=0, tiled=True),
        lax.psum_scatter(key_part, ("seq", "dp"), scatter_dimension=0, tiled=True),
        lax.psum_scatter(value_part, ("seq", "dp"), scatter_dimension=0, tiled=True),
        lax.psum_scatter(outproj_part, ("seq", "dp"), scatter_dimension=0, tiled=True),
        lax.psum_scatter(relative_part, ("seq", "dp"), scatter_dimension=0, tiled=True),
        lax.psum_scatter(crossquery_part, ("seq", "dp"), scatter_dimension=0, tiled=True),
        lax.psum_scatter(crosskey_part, ("seq", "dp"), scatter_dimension=0, tiled=True),
        lax.psum_scatter(crossvalue_part, ("seq", "dp"), scatter_dimension=0, tiled=True),
        lax.psum_scatter(crossout_part, ("seq", "dp"), scatter_dimension=0, tiled=True),
        lax.psum_scatter(up_part, ("seq", "dp"), scatter_dimension=0, tiled=True),
        lax.psum_scatter(down_part, ("seq", "dp"), scatter_dimension=0, tiled=True),
        lax.psum_scatter(gainattn_part, ("seq", "dp"), scatter_dimension=0, tiled=True),
        lax.psum_scatter(gaincross_part, ("seq", "dp"), scatter_dimension=0, tiled=True),
        lax.psum_scatter(gainffn_part, ("seq", "dp"), scatter_dimension=0, tiled=True),
    )
    return (
        result.astype(jnp.bfloat16),
        hidden_grad,
        encoder_grad,
        query_sum,
        keyw_sum,
        valuew_sum,
        outproj_sum,
        relative_sum,
        cquery_sum,
        ckey_sum,
        cvalue_sum,
        cout_sum,
        up_sum,
        down_sum,
        gainattn_sum,
        gaincross_sum,
        gainffn_sum,
    )


def solution(mesh):
    in_specs = (
        P(None, "dp", "seq", None),
        P("dp", "seq", None),
        P("dp"),
        P("dp"),
        P("dp", None),
        P("dp", None),
        P("dp", None),
        P("dp", None),
        P("dp", None),
        P("dp", None),
        P("dp", None),
        P("dp", None),
        P("dp", None),
        P("dp", None),
        P("dp", None),
        P("dp"),
        P("dp"),
        P("dp"),
        P(None, "dp", "seq", None),
    )
    out_specs = (
        P(None, "dp", "seq", None),
        P(None, "dp", "seq", None),
        P("dp", "seq", None),
        P(("seq", "dp"), None),
        P(("seq", "dp"), None),
        P(("seq", "dp"), None),
        P(("seq", "dp"), None),
        P(("seq", "dp"), None),
        P(("seq", "dp"), None),
        P(("seq", "dp"), None),
        P(("seq", "dp"), None),
        P(("seq", "dp"), None),
        P(("seq", "dp"), None),
        P(("seq", "dp"), None),
        P(("seq", "dp")),
        P(("seq", "dp")),
        P(("seq", "dp")),
    )
    return jax.shard_map(local, mesh=mesh, in_specs=in_specs, out_specs=out_specs, check_vma=False)
```

profile of v0, /device:TPU:0, one launch (start us, length us, event | category | flops | bytes accessed | tf_op | source)
XLA Modules:
  0.0 2422.1 jit_solution(18053097824848890559)
XLA Ops:
  11.2 30.3 %all-gather.23.cloned.1.call-done = bf16[1024,1024]{1,0:T(8,128)(2,1)} async-done(((bf16[128,1024]{1,0:T(8,128)(2,1)}), bf16[1024,1024]{1,0:T(8,128)(2,1)}) %all-gather.23.cloned.1.call-update) | async-done | bytes 2097168 | tf_op jit(solution)/shard_map/all_gather | solution.py:130
  46.0 25.7 %all-gather.21.cloned.1.call-done = bf16[1024,1024]{1,0:T(8,128)(2,1)} async-done(((bf16[128,1024]{1,0:T(8,128)(2,1)}), bf16[1024,1024]{1,0:T(8,128)(2,1)}) %all-gather.21.cloned.1.call-update) | async-done | bytes 2097168 | tf_op jit(solution)/shard_map/all_gather | solution.py:131
  77.3 24.7 %all-gather.35.cloned.1.call-done = bf16[1024,1024]{1,0:T(8,128)(2,1)} async-done(((bf16[128,1024]{1,0:T(8,128)(2,1)}), bf16[1024,1024]{1,0:T(8,128)(2,1)}) %all-gather.35.cloned.1.call-update) | async-done | bytes 2097168 | tf_op jit(solution)/shard_map/all_gather | solution.py:135
  104.8 27.2 %all-gather.31.cloned.1.call-done = bf16[1024,1024]{1,0:T(8,128)(2,1)} async-done(((bf16[128,1024]{1,0:T(8,128)(2,1)}), bf16[1024,1024]{1,0:T(8,128)(2,1)}) %all-gather.31.cloned.1.call-update) | async-done | bytes 2097168 | tf_op jit(solution)/shard_map/all_gather | solution.py:136
  200.5 12.8 all-gather.49.cloned.1.call-done
  214.8 27.6 %all-gather.47.cloned.1.call-done = bf16[1,2,256,1024]{3,2,1,0:T(8,128)(2,1)} async-done(((bf16[1,2,64,1024]{3,2,1,0:T(8,128)(2,1)}), bf16[1,2,256,1024]{3,2,1,0:T(8,128)(2,1)}) %all-gather.47.cloned.1.call-update) | async-done | bytes 1048592 | tf_op jit(solution)/shard_map/all_gather | solution.py:158
  277.5 25.6 %all-gather.39.cloned.1.call-done = bf16[1024,1024]{1,0:T(8,128)(2,1)} async-done(((bf16[128,1024]{1,0:T(8,128)(2,1)}), bf16[1024,1024]{1,0:T(8,128)(2,1)}) %all-gather.39.cloned.1.call-update) | async-done | bytes 2097168 | tf_op jit(solution)/shard_map/all_gather | solution.py:134
  311.9 19.9 all-gather.37.cloned.1.call-done
  334.0 26.7 %all-gather.33.cloned.1.call-done = bf16[2,256,1024]{2,1,0:T(8,128)(2,1)} async-done(((bf16[2,64,1024]{2,1,0:T(8,128)(2,1)}), bf16[2,256,1024]{2,1,0:T(8,128)(2,1)}) %all-gather.33.cloned.1.call-update) | async-done | bytes 1048592 | tf_op jit(solution)/shard_map/all_gather | solution.py:160
  396.5 77.9 %all-gather.43.cloned.1.call-done = bf16[1024,4096]{1,0:T(8,128)(2,1)} async-done(((bf16[128,4096]{1,0:T(8,128)(2,1)}), bf16[1024,4096]{1,0:T(8,128)(2,1)}) %all-gather.43.cloned.1.call-update) | async-done | bytes 8388624 | tf_op jit(solution)/shard_map/all_gather | solution.py:138
  485.7 15.4 multiply_convert_fusion
  501.2 55.3 %all-gather.45.cloned.1.call-done = bf16[4096,1024]{1,0:T(8,128)(2,1)} async-done(((bf16[512,1024]{1,0:T(8,128)(2,1)}), bf16[4096,1024]{1,0:T(8,128)(2,1)}) %all-gather.45.cloned.1.call-update) | async-done | bytes 8388624 | tf_op jit(solution)/shard_map/all_gather | solution.py:139
  566.6 14.3 add_convert_fusion
  841.0 39.2 %all-reduce.3 = (f32[1024]{0:T(1024)S(1)}, f32[1024]{0:T(1024)S(1)}, f32[1024]{0:T(1024)S(1)}) all-reduce(f32[1024]{0:T(1024)S(1)} %copy-done.109, f32[1024]{0:T(1024)S(1)} %copy-done.108, f32[1024]{0:T(1024)S(1)} %copy-done.98), channel_id=19, replica_groups=mesh['seq'=4,'dp'=8] {'seq','dp'}, use_global_device_ids=true, to_apply=%region_39.40.clone | all-reduce | flops 3072 | bytes 24576
  902.0 142.1 %reduce-scatter.40.cloned.1.call-done = f32[32,1024]{1,0:T(8,128)} async-done(((f32[1024,1024]{1,0:T(8,128)}), f32[32,1024]{1,0:T(8,128)}) %reduce-scatter.40.cloned.1.call-update) | async-done | bytes 131088 | tf_op jit(solution)/shard_map/reduce_scatter | solution.py:339
  1044.1 142.5 %reduce-scatter.36.cloned.1.call-done = f32[32,1024]{1,0:T(8,128)} async-done(((f32[1024,1024]{1,0:T(8,128)}), f32[32,1024]{1,0:T(8,128)}) %reduce-scatter.36.cloned.1.call-update) | async-done | bytes 131088 | tf_op jit(solution)/shard_map/reduce_scatter | solution.py:334
  1186.6 142.4 %reduce-scatter.54.cloned.1.call-done = f32[32,1024]{1,0:T(8,128)} async-done(((f32[1024,1024]{1,0:T(8,128)}), f32[32,1024]{1,0:T(8,128)}) %reduce-scatter.54.cloned.1.call-update) | async-done | bytes 131088
  1329.0 142.3 %reduce-scatter.38.cloned.1.call-done = f32[32,1024]{1,0:T(8,128)} async-done(((f32[1024,1024]{1,0:T(8,128)}), f32[32,1024]{1,0:T(8,128)}) %reduce-scatter.38.cloned.1.call-update) | async-done | bytes 131088 | tf_op jit(solution)/shard_map/reduce_scatter | solution.py:336
  1471.2 142.7 %reduce-scatter.58.cloned.1.call-done = f32[32,1024]{1,0:T(8,128)} async-done(((f32[1024,1024]{1,0:T(8,128)}), f32[32,1024]{1,0:T(8,128)}) %reduce-scatter.58.cloned.1.call-update) | async-done | bytes 131088
  1614.0 142.4 %reduce-scatter.56.cloned.1.call-done = f32[32,1024]{1,0:T(8,128)} async-done(((f32[1024,1024]{1,0:T(8,128)}), f32[32,1024]{1,0:T(8,128)}) %reduce-scatter.56.cloned.1.call-update) | async-done | bytes 131088
  1756.3 142.3 %reduce-scatter.62.cloned.1.call-done = f32[32,1024]{1,0:T(8,128)} async-done(((f32[1024,1024]{1,0:T(8,128)}), f32[32,1024]{1,0:T(8,128)}) %reduce-scatter.62.cloned.1.call-update) | async-done | bytes 131088
  1898.6 142.7 %reduce-scatter.64.cloned.1.call-done = f32[32,1024]{1,0:T(8,128)} async-done(((f32[1024,1024]{1,0:T(8,128)}), f32[32,1024]{1,0:T(8,128)}) %reduce-scatter.64.cloned.1.call-update) | async-done | bytes 131088
  2041.2 186.6 %reduce-scatter.44.cloned.1.call-done = f32[128,1024]{1,0:T(8,128)} async-done(((f32[4096,1024]{1,0:T(8,128)}), f32[128,1024]{1,0:T(8,128)}) %reduce-scatter.44.cloned.1.call-update) | async-done | bytes 524304 | tf_op jit(solution)/shard_map/reduce_scatter | solution.py:341
  2227.8 187.2 %reduce-scatter.42.cloned.1.call-done = f32[32,4096]{1,0:T(8,128)} async-done(((f32[1024,4096]{1,0:T(8,128)}), f32[32,4096]{1,0:T(8,128)}) %reduce-scatter.42.cloned.1.call-update) | async-done | bytes 524304 | tf_op jit(solution)/shard_map/reduce_scatter | solution.py:340
  (500 shorter events, 470.1 us)
Async XLA Ops:
  10.0 158.2 %all-gather.27.cloned.1.call-start = ((), (), s32[]{:S(2)}) async-start(), calls=%async_computation.18 | async-start | bytes 1179648 | tf_op jit(solution)/shard_map/all_gather | solution.py:133
  10.6 174.7 %all-gather.25.cloned.1.call-start = ((), (), s32[]{:S(2)}) async-start(), calls=%async_computation.17 | async-start | bytes 2359296 | tf_op jit(solution)/shard_map/all_gather | solution.py:129
  11.2 202.1 %all-gather.49.cloned.1.call-start = ((), (), s32[]{:S(2)}) async-start(), calls=%async_computation.34 | async-start | bytes 1310720 | tf_op jit(solution)/shard_map/all_gather | solution.py:157
  45.9 196.4 %all-gather.47.cloned.1.call-start = ((), (), s32[]{:S(2)}) async-start(), calls=%async_computation.33 | async-start | bytes 1310720 | tf_op jit(solution)/shard_map/all_gather | solution.py:158
  75.9 197.2 %all-gather.29.cloned.1.call-start = ((), (), s32[]{:S(2)}) async-start(), calls=%async_computation.19 | async-start | bytes 2359296 | tf_op jit(solution)/shard_map/all_gather | solution.py:132
  76.6 226.5 %all-gather.39.cloned.1.call-start = ((), (), s32[]{:S(2)}) async-start(), calls=%async_computation.24 | async-start | bytes 2359296 | tf_op jit(solution)/shard_map/all_gather | solution.py:134
  77.2 254.5 %all-gather.37.cloned.1.call-start = ((), (), s32[]{:S(2)}) async-start(), calls=%async_computation.23 | async-start | bytes 1310720 | tf_op jit(solution)/shard_map/all_gather | solution.py:159
  104.8 255.9 %all-gather.33.cloned.1.call-start = ((), (), s32[]{:S(2)}) async-start(), calls=%async_computation.21 | async-start | bytes 1310720 | tf_op jit(solution)/shard_map/all_gather | solution.py:160
  134.8 256.6 %all-gather.41.cloned.1.call-start = ((), (), s32[]{:S(2)}) async-start(), calls=%async_computation.25 | async-start | bytes 2359296 | tf_op jit(solution)/shard_map/all_gather | solution.py:137
  135.5 338.9 %all-gather.43.cloned.1.call-start = ((), (), s32[]{:S(2)}) async-start(), calls=%async_computation.26 | async-start | bytes 9437184 | tf_op jit(solution)/shard_map/all_gather | solution.py:138
  136.1 420.4 %all-gather.45.cloned.1.call-start = ((), (), s32[]{:S(2)}) async-start(), calls=%async_computation.27 | async-start | bytes 9437184 | tf_op jit(solution)/shard_map/all_gather | solution.py:139
  136.7 625.3 %reduce-scatter.48.cloned.1.call-start = ((), (), s32[]{:S(2)}) async-start(), calls=%async_computation.36 | async-start | bytes 1310720
  643.8 136.3 %reduce-scatter.46.cloned.1.call-start = ((), (), s32[]{:S(2)}) async-start(), calls=%async_computation.35 | async-start | bytes 1310720
  698.9 203.1 %reduce-scatter.60.cloned.1.call-start = ((), (), s32[]{:S(2)}) async-start(), calls=%async_computation.42 | async-start | bytes 2162688
  717.7 326.4 %reduce-scatter.40.cloned.1.call-start = ((), (), s32[]{:S(2)}) async-start(), calls=%async_computation.30 | async-start | bytes 4325376 | tf_op jit(solution)/shard_map/reduce_scatter | solution.py:339
  723.3 463.3 %reduce-scatter.36.cloned.1.call-start = ((), (), s32[]{:S(2)}) async-start(), calls=%async_computation.28 | async-start | bytes 4325376 | tf_op jit(solution)/shard_map/reduce_scatter | solution.py:334
  728.4 600.6 %reduce-scatter.54.cloned.1.call-start = ((), (), s32[]{:S(2)}) async-start(), calls=%async_computation.39 | async-start | bytes 4325376
  748.6 722.6 %reduce-scatter.38.cloned.1.call-start = ((), (), s32[]{:S(2)}) async-start(), calls=%async_computation.29 | async-start | bytes 4325376 | tf_op jit(solution)/shard_map/reduce_scatter | solution.py:336
  756.5 857.5 %reduce-scatter.58.cloned.1.call-start = ((), (), s32[]{:S(2)}) async-start(), calls=%async_computation.41 | async-start | bytes 4325376
  774.4 981.9 %reduce-scatter.56.cloned.1.call-start = ((), (), s32[]{:S(2)}) async-start(), calls=%async_computation.40 | async-start | bytes 4325376
  792.5 1106.1 %reduce-scatter.62.cloned.1.call-start = ((), (), s32[]{:S(2)}) async-start(), calls=%async_computation.43 | async-start | bytes 4325376
  802.8 1238.4 %reduce-scatter.64.cloned.1.call-start = ((), (), s32[]{:S(2)}) async-start(), calls=%async_computation.44 | async-start | bytes 4325376
  813.2 1414.6 %reduce-scatter.44.cloned.1.call-start = ((), (), s32[]{:S(2)}) async-start(), calls=%async_computation.32 | async-start | bytes 17301504 | tf_op jit(solution)/shard_map/reduce_scatter | solution.py:341
  827.4 1587.6 %reduce-scatter.42.cloned.1.call-start = ((), (), s32[]{:S(2)}) async-start(), calls=%async_computation.31 | async-start | bytes 17301504 | tf_op jit(solution)/shard_map/reduce_scatter | solution.py:340
  (136 other events, 2221.7 us)
Sparse Core Ops, SparseCore 0:
  9.6 31.7 all-gather.22
  43.1 28.5 all-gather.20
  73.3 28.5 all-gather.34
  103.4 28.5 all-gather.30
  156.6 28.6 all-gather.24
  243.9 29.0 all-gather.28
  274.5 28.5 all-gather.38
  362.3 29.0 all-gather.40
  392.8 81.5 all-gather.42
  475.9 80.5 all-gather.44
  673.3 27.6 reduce-scatter.45
  703.7 27.7 reduce-scatter.49
  734.6 27.7 reduce-scatter.51
  765.1 136.8 reduce-scatter.59
  904.9 139.1 reduce-scatter.39
  1047.1 139.4 reduce-scatter.35
  1189.6 139.3 reduce-scatter.53
  1331.8 139.4 reduce-scatter.37
  1474.2 139.7 reduce-scatter.57
  1616.8 139.5 reduce-scatter.55
  1759.1 139.4 reduce-scatter.61
  1901.5 139.6 reduce-scatter.63
  2044.2 183.5 reduce-scatter.43
  2230.6 184.3 reduce-scatter.41
  (6 shorter events, 153.0 us)
where the time goes:
time: 2430 us; the launch traced here: 2420 us
  waiting for transfers between devices  1900 us (78%)
  matrix products  193 us (8%)
  local copies, waits for them, and re-layouts  175 us (7%)
  blocking collectives  68.2 us (3%)
  other arithmetic  64.9 us (3%)
    unnamed x40, waiting for transfers between devices  727 us
    reduce_scatter x1, waiting for transfers between devices, local(): lax.psum_scatter(up_part, ('seq', 'dp'), scatter_dimension=0, tiled=True)  187 us
    reduce_scatter x1, waiting for transfers between devices, local(): lax.psum_scatter(down_part, ('seq', 'dp'), scatter_dimension=0, tiled=True)  187 us
    reduce_scatter x1, waiting for transfers between devices, local(): lax.psum_scatter(outproj_part, ('seq', 'dp'), scatter_dimension=0, tiled=...  142 us
    reduce_scatter x1, waiting for transfers between devices, local(): lax.psum_scatter(crossquery_part, ('seq', 'dp'), scatter_dimension=0, til...  142 us
    reduce_scatter x1, waiting for transfers between devices, local(): lax.psum_scatter(crossout_part, ('seq', 'dp'), scatter_dimension=0, tiled...  142 us
    unnamed x285, local copies, waits for them, and re-layouts  98.9 us
    all_gather x1, waiting for transfers between devices, local(): lax.all_gather(w_up, 'dp', axis=0, tiled=True)  77.9 us
  transfers between devices with their start and end apart: 30, of which 25 were waited for; matrix products, arithmetic and copies ran while one was open for 13% of the time, Pallas kernels for 0%

commit v1 on v0

--- a/solution.py
+++ b/solution.py
@@ -3,7 +3,11 @@
 import jax
 import jax.numpy as jnp
 from jax import lax
+from jax.experimental import pallas as pl
+from jax.experimental.pallas import tpu as pltpu
 from jax.sharding import PartitionSpec as P
+
+MESH = pl.DeviceIdType.MESH
 
 HEADS = 16
 HEAD_DIM = 64
@@ -87,6 +91,332 @@
 
 def turned(array):
     return jnp.transpose(array, (0, 1, 3, 2))
+
+
+def remote(src, dst, send, recv, to):
+    return pltpu.make_async_remote_copy(
+        src_ref=src, dst_ref=dst, send_sem=send, recv_sem=recv, device_id=to, device_id_type=MESH
+    )
+
+
+def place():
+    s = lax.axis_index("seq")
+    d = lax.axis_index("dp")
+    z, c = d // 2, lax.rem(d, 2)
+    sx = s + 1 - 2 * lax.rem(s, 2)
+    sy = lax.rem(s + 2, 4)
+    return s, z, c, sx, sy
+
+
+def greet(nz):
+    s, z, c, sx, sy = place()
+    barrier = pltpu.get_barrier_semaphore()
+    dests = [(s, 2 * z + 1 - c), (sx, 2 * z + c), (sy, 2 * z + c)]
+    for dz in range(1, nz):
+        dests.append((s, 2 * lax.rem(z + dz, nz) + c))
+    for dest in dests:
+        pl.semaphore_signal(barrier, inc=1, device_id=dest, device_id_type=MESH)
+    pl.semaphore_wait(barrier, len(dests))
+
+
+def gather_weights_kernel(count, nz, *refs):
+    shards, wholes = refs[:count], refs[count : 2 * count]
+    local_sem, send, recv = refs[2 * count :]
+    s, z, c, sx, sy = place()
+    own = 2 * z + c
+    core = (s, 2 * z + 1 - c)
+    beside_x, beside_y = (sx, own), (sy, own)
+    greet(nz)
+    started = []
+
+    def put(copy):
+        copy.start()
+        started.append(copy)
+
+    def rows_of(i, q, half):
+        quarter = shards[i].shape[0] // 4
+        if half is None:
+            return pl.ds(q * quarter, quarter)
+        return pl.ds(q * quarter + half * (quarter // 2), quarter // 2)
+
+    split = [shards[i].shape[0] % 128 == 0 for i in range(count)]
+    def along_z(i):
+        here = pltpu.make_async_copy(shards[i], wholes[i].at[own], local_sem.at[i])
+        here.start()
+        started.append(here)
+        for dz in range(1, nz):
+            to = (s, 2 * lax.rem(z + dz, nz) + c)
+            if split[i]:
+                src, dst = shards[i].at[rows_of(i, s, None)], wholes[i].at[own, rows_of(i, s, None)]
+            else:
+                src, dst = shards[i], wholes[i].at[own]
+            put(remote(src, dst, send.at[i, dz, 0], recv.at[i, dz, 0], to))
+        put(remote(shards[i], wholes[i].at[own], send.at[i, 0, 0], recv.at[i, 0, 0], core))
+
+    def moved(i, dz, kind, q, half, to):
+        block = 2 * lax.rem(z + nz - dz, nz) + c
+        part = wholes[i].at[block, rows_of(i, q, half)] if split[i] else wholes[i].at[block]
+        return remote(part, part, send.at[i, dz, kind], recv.at[i, dz, kind], to)
+
+    def to_core(i, dz, kind, q, half):
+        put(moved(i, dz, kind, q, half, core))
+
+    def first(i):
+        for dz in range(1, nz):
+            moved(i, dz, 0, s, None, core).wait_recv()
+            if split[i]:
+                put(moved(i, dz, 1, s, None, beside_x))
+                put(moved(i, dz, 2, s, None, beside_y))
+            to_core(i, dz, 5, s, None)
+
+    def second(i):
+        if not split[i]:
+            return
+        for dz in range(1, nz):
+            moved(i, dz, 1, sx, None, core).wait_recv()
+            put(moved(i, dz, 4, sx, 0, beside_y))
+            to_core(i, dz, 6, sx, None)
+            moved(i, dz, 2, sy, None, core).wait_recv()
+            put(moved(i, dz, 3, sy, 1, beside_x))
+            to_core(i, dz, 7, sy, None)
+
+    def third(i):
+        if not split[i]:
+            return
+        for dz in range(1, nz):
+            moved(i, dz, 4, 3 - s, 0, core).wait_recv()
+            to_core(i, dz, 8, 3 - s, 0)
+            moved(i, dz, 3, 3 - s, 1, core).wait_recv()
+            to_core(i, dz, 9, 3 - s, 1)
+
+    def last(i):
+        other = 1 - c
+        block = wholes[i].at[2 * z + other]
+        remote(block, block, send.at[i, 0, 0], recv.at[i, 0, 0], core).wait_recv()
+        for dz in range(1, nz):
+            block = wholes[i].at[2 * lax.rem(z + nz - dz, nz) + other]
+            kinds = [(5, s, None)]
+            if split[i]:
+                kinds += [(6, sx, None), (7, sy, None), (8, 3 - s, 0), (9, 3 - s, 1)]
+            for kind, q, half in kinds:
+                part = block.at[rows_of(i, q, half)] if split[i] else block
+                remote(part, part, send.at[i, dz, kind], recv.at[i, dz, kind], core).wait_recv()
+
+    ahead = 3
+    for i in range(min(ahead, count)):
+        along_z(i)
+    for i in range(count + 2):
+        if i < count:
+            first(i)
+        if ahead + i < count:
+            along_z(ahead + i)
+        if 1 <= i <= count:
+            second(i - 1)
+        if i >= 2:
+            third(i - 2)
+    for i in range(count):
+        last(i)
+    for copy in started:
+        if hasattr(copy, "wait_send") and copy.is_remote:
+            copy.wait_send()
+        else:
+            copy.wait()
+
+
+def gather_weights(shards, ndp):
+    nz = ndp // 2
+    count = len(shards)
+    return pl.pallas_call(
+        lambda *refs: gather_weights_kernel(count, nz, *refs),
+        out_shape=[jax.ShapeDtypeStruct((ndp,) + w.shape, w.dtype) for w in shards],
+        in_specs=[pl.BlockSpec(memory_space=pl.ANY)] * count,
+        out_specs=[pl.BlockSpec(memory_space=pl.ANY)] * count,
+        scratch_shapes=[
+            pltpu.SemaphoreType.DMA((count,)),
+            pltpu.SemaphoreType.DMA((count, nz, 10)),
+            pltpu.SemaphoreType.DMA((count, nz, 10)),
+        ],
+        compiler_params=pltpu.CompilerParams(collective_id=0, has_side_effects=True),
+        name="gather_weights",
+    )(*shards)
+
+
+def reduce_grads_kernel(plan, nz, n_x, n_g, n_out, *refs):
+    at = 0
+    xs, at = refs[at : at + n_x], at + n_x
+    gs, at = refs[at : at + n_g], at + n_g
+    gain_part, at = refs[at], at + 1
+    outs, at = refs[at : at + n_out], at + n_out
+    gain_out, at = refs[at], at + 1
+    kinds = []
+    for _ in range(3):
+        kinds.append(refs[at : at + 5])
+        at += 5
+    send, recv = refs[at : at + 2]
+    s, z, c, sx, sy = place()
+    own = 2 * z + c
+    x, y = lax.rem(s, 2), s // 2
+    core = (s, 2 * z + 1 - c)
+    beside_x, beside_y = (sx, own), (sy, own)
+    greet(nz)
+    count = len(plan)
+
+    def buffers(k):
+        kind, slot = plan[k][0], plan[k][1]
+        part, held0, held1, held2, held3 = kinds[kind]
+        if kind == 2:
+            return gain_part, held0.at[slot], held1.at[slot], held2.at[slot], held3.at[slot]
+        return (part.at[slot % 2], held0.at[slot], held1.at[slot], held2.at[slot], held3.at[slot])
+
+    def core_copy(k):
+        part, held0 = buffers(k)[:2]
+        return remote(part.at[:, :, :, 1 - c], held0, send.at[k, 0], recv.at[k, 0], core)
+
+    def first_copy(k):
+        _, held0, held1 = buffers(k)[:3]
+        if k % 2 == 0:
+            return remote(held0.at[:, 1 - x], held1, send.at[k, 1], recv.at[k, 1], beside_x)
+        return remote(held0.at[1 - y], held1, send.at[k, 1], recv.at[k, 1], beside_y)
+
+    def second_copy(k):
+        held1, held2 = buffers(k)[2:4]
+        if k % 2 == 0:
+            return remote(held1.at[1 - y], held2, send.at[k, 2], recv.at[k, 2], beside_y)
+        return remote(held1.at[1 - x], held2, send.at[k, 2], recv.at[k, 2], beside_x)
+
+    def z_copy(k, dz):
+        held2, held3 = buffers(k)[3:5]
+        zt = lax.rem(z + dz, nz)
+        return remote(
+            held2.at[zt], held3.at[dz - 1], send.at[k, 2 + dz], recv.at[k, 2 + dz], (s, 2 * zt + c)
+        )
+
+    def added(held, mine):
+        held[...] = (held[...].astype(jnp.float32) + mine.astype(jnp.float32)).astype(held.dtype)
+
+    def make(k):
+        kind, slot, xi, gi, _, col, wide = plan[k]
+        if kind < 2:
+            part = buffers(k)[0]
+            left, right = xs[xi], gs[gi]
+            block = part.shape[4]
+            if slot >= 2:
+                core_copy(before[k]).wait_send()
+            group = 256 // block
+            for i in range(left.shape[1] // 256):
+                product = lax.dot_general(
+                    left[:, i * 256 : (i + 1) * 256],
+                    right[:, col : col + wide],
+                    (((0,), (0,)), ((), ())),
+                    preferred_element_type=jnp.float32,
+                )
+                index = i * group
+                i_s, rest = divmod(index, 2 * nz)
+                zs = rest // 2
+                part[i_s // 2, i_s % 2, zs : zs + group // 2] = product.reshape(group // 2, 2, block, wide).astype(
+                    part.dtype
+                )
+        core_copy(k).start()
+
+    def after_core(k):
+        part, held0 = buffers(k)[:2]
+        core_copy(k).wait_recv()
+        added(held0, part[:, :, :, c])
+        first_copy(k).start()
+
+    def after_first(k):
+        _, held0, held1 = buffers(k)[:3]
+        first_copy(k).wait_recv()
+        added(held1, held0[:, x] if k % 2 == 0 else held0[y])
+        second_copy(k).start()
+
+    def after_second(k):
+        held1, held2 = buffers(k)[2:4]
+        second_copy(k).wait_recv()
+        added(held2, held1[y] if k % 2 == 0 else held1[x])
+        for dz in range(1, nz):
+            z_copy(k, dz).start()
+
+    def finish(k):
+        held2, held3 = buffers(k)[3:5]
+        total = held2[z].astype(jnp.float32)
+        for dz in range(1, nz):
+            z_copy(k, dz).wait_recv()
+            total = total + held3[dz - 1].astype(jnp.float32)
+        kind, _, _, _, oi, col, wide = plan[k]
+        if kind == 2:
+            gain_out[...] = total
+        else:
+            outs[oi][:, col : col + wide] = total
+
+    before = {}
+    recent = {}
+    for k in range(count):
+        kind, slot = plan[k][0], plan[k][1]
+        before[k] = recent.get((kind, slot - 2))
+        recent[(kind, slot)] = k
+    followed = set(v for v in before.values() if v is not None)
+
+    for t in range(count + 7):
+        if t >= 7:
+            finish(t - 7)
+        if 5 <= t < count + 5:
+            after_second(t - 5)
+        if 3 <= t < count + 3:
+            after_first(t - 3)
+        if t < count:
+            make(t)
+        if 1 <= t < count + 1:
+            after_core(t - 1)
+    for k in range(count):
+        if k not in followed:
+            core_copy(k).wait_send()
+        first_copy(k).wait_send()
+        second_copy(k).wait_send()
+        for dz in range(1, nz):
+            z_copy(k, dz).wait_send()
+
+
+def reduce_grads(xs, gs, pairs, gain_part, nz):
+    plan, slots = [], [0, 0, 0]
+    blocks, columns = [], []
+    ndev = 8 * nz
+    for oi, (xi, gi) in enumerate(pairs):
+        rows, wide = xs[xi].shape[1], gs[gi].shape[1]
+        columns.append((rows // ndev, wide))
+        kind = 0 if rows // ndev <= 32 else 1
+        step = (512, 256)[kind]
+        for col in range(0, wide, step):
+            plan.append((kind, slots[kind], xi, gi, oi, col, step))
+            slots[kind] += 1
+    plan.append((2, 0, 0, 0, 0, 0, 128))
+    rb = min(rows for rows, _ in columns)
+    shapes = [((rb, 512), jnp.bfloat16, slots[0]), ((max(rows for rows, _ in columns), 256), jnp.bfloat16, slots[1])]
+    scratch = []
+    for (tail, kind_type, n) in shapes + [((8, 128), jnp.float32, 1)]:
+        scratch.append(
+            pltpu.VMEM((2, 2, 2, nz, 2) + tail if kind_type == jnp.bfloat16 else (8, 128), kind_type)
+        )
+        scratch.append(pltpu.VMEM((n, 2, 2, nz) + tail, kind_type))
+        scratch.append(pltpu.VMEM((n, 2, nz) + tail, kind_type))
+        scratch.append(pltpu.VMEM((n, nz) + tail, kind_type))
+        scratch.append(pltpu.VMEM((n, nz - 1) + tail, kind_type))
+    n = len(plan)
+    vmem = pl.BlockSpec(memory_space=pltpu.VMEM)
+    outs = [jax.ShapeDtypeStruct(shape, jnp.float32) for shape in columns]
+    outs.append(jax.ShapeDtypeStruct((8, 128), jnp.float32))
+    return pl.pallas_call(
+        lambda *refs: reduce_grads_kernel(plan, nz, len(xs), len(gs), len(columns), *refs),
+        out_shape=outs,
+        in_specs=[vmem] * (len(xs) + len(gs) + 1),
+        out_specs=[vmem] * len(outs),
+        scratch_shapes=scratch
+        + [pltpu.SemaphoreType.DMA((n, 2 + nz)), pltpu.SemaphoreType.DMA((n, 2 + nz))],
+        compiler_params=pltpu.CompilerParams(
+            collective_id=1, has_side_effects=True, vmem_limit_bytes=62 * 2**20
+        ),
+        name="reduce_grads",
+    )(*xs, *gs, gain_part)
 
 
 def local(
@@ -110,37 +440,46 @@
     gain_ffn,
     cotangent,
 ):
+    ndp = lax.axis_size("dp")
+    devices = ndp * lax.axis_size("seq")
+    weights = (
+        w_key,
+        w_value,
+        w_query,
+        w_relative,
+        w_attn_out,
+        w_cross_key,
+        w_cross_value,
+        w_cross_query,
+        w_cross_out,
+        w_up,
+        w_down,
+    )
+    gains = jnp.stack([gain_attn, gain_cross, gain_ffn])
+    kernels = lax.axis_size("seq") == 4 and w_query.shape[0] % 128 == 0
+    if kernels:
+        gains = jnp.pad(gains, ((0, 13), (0, 0)))
+        *whole, whole_gains = gather_weights(weights + (gains,), ndp)
+        whole = [w.reshape(-1, w.shape[-1]) for w in whole]
+        whole_gains = whole_gains[:, :3]
+    else:
+        whole = [lax.all_gather(w, "dp", axis=0, tiled=True) for w in weights]
+        whole_gains = lax.all_gather(gains, "dp", axis=0)
+    whole_gains = jnp.transpose(whole_gains, (1, 0, 2)).reshape(3, -1)
+    full_gain_attn, full_gain_cross, full_gain_ffn = whole_gains
     (
-        full_query,
         full_key,
         full_value,
+        full_query,
+        full_relative,
         full_attn_out,
-        full_relative,
-        full_cquery,
         full_ckey,
         full_cvalue,
+        full_cquery,
         full_cout,
         full_up,
         full_down,
-        full_gain_attn,
-        full_gain_cross,
-        full_gain_ffn,
-    ) = (
-        lax.all_gather(w_query, "dp", axis=0, tiled=True),
-        lax.all_gather(w_key, "dp", axis=0, tiled=True),
-        lax.all_gather(w_value, "dp", axis=0, tiled=True),
-        lax.all_gather(w_attn_out, "dp", axis=0, tiled=True),
-        lax.all_gather(w_relative, "dp", axis=0, tiled=True),
-        lax.all_gather(w_cross_query, "dp", axis=0, tiled=True),
-        lax.all_gather(w_cross_key, "dp", axis=0, tiled=True),
-        lax.all_gather(w_cross_value, "dp", axis=0, tiled=True),
-        lax.all_gather(w_cross_out, "dp", axis=0, tiled=True),
-        lax.all_gather(w_up, "dp", axis=0, tiled=True),
-        lax.all_gather(w_down, "dp", axis=0, tiled=True),
-        lax.all_gather(gain_attn, "dp", axis=0, tiled=True),
-        lax.all_gather(gain_cross, "dp", axis=0, tiled=True),
-        lax.all_gather(gain_ffn, "dp", axis=0, tiled=True),
-    )
+    ) = whole
     streams, row_count, local_len, width = hidden.shape
     enc_local = encoder.shape[1]
     seq_len = local_len * lax.axis_size("seq")
@@ -219,14 +558,11 @@
     result, norm_ffn_pull = jax.vjp(layer_norm, crossed + down, full_gain_ffn.astype(jnp.float32))
     ffn_grad, gainffn_part = norm_ffn_pull(cotangent.astype(jnp.float32))
     down_low = ffn_grad.astype(jnp.bfloat16)
-    down_part = weight_grad(activated_low, down_low)
     (upward_grad,) = gelu_pull(project_back(down_low, full_down))
     upward_low = upward_grad.astype(jnp.bfloat16)
-    up_part = weight_grad(crossed_low, upward_low)
     crossed_grad = ffn_grad + project_back(upward_low, full_up)
     cross_res_grad, gaincross_part = norm_cross_pull(crossed_grad)
     cross_res_low = cross_res_grad.astype(jnp.bfloat16)
-    crossout_part = weight_grad(cross_context_low, cross_res_low)
     cross_ctx_grad = project_back(cross_res_low, full_cout).astype(jnp.bfloat16).reshape(head_shape)
     cross_prob_grad = jnp.einsum(
         "jrthe,rshe->jrhts", cross_ctx_grad, all_enc_values, preferred_element_type=jnp.float32
@@ -244,10 +580,8 @@
     )
     cross_query_back = (cross_query_grad.astype(jnp.bfloat16) * 0.125).reshape(flat_shape)
     normed_grad = cross_res_grad + project_back(cross_query_back, full_cquery)
-    crossquery_part = weight_grad(normed_low, cross_query_back)
     residual_grad, gainattn_part = norm_attn_pull(normed_grad)
     attn_low = residual_grad.astype(jnp.bfloat16)
-    outproj_part = weight_grad(context_low, attn_low)
     context_grad = project_back(attn_low, full_attn_out).astype(jnp.bfloat16).reshape(head_shape)
     main_prob_grad = jnp.einsum(
         "jrthe,rshe->jrhts", context_grad, all_values, preferred_element_type=jnp.float32
@@ -306,43 +640,64 @@
     hidden_grad = (
         hidden_grad + project_back(value_back, full_value) + project_back(rel_back, full_relative)
     )
-    query_part = weight_grad(hidden, query_back)
-    key_part = weight_grad(hidden, key_back)
-    value_part = weight_grad(hidden, value_back)
-    relative_part = weight_grad(hidden, rel_back)
-    crosskey_part = weight_grad(encoder, enc_key_back)
-    crossvalue_part = weight_grad(encoder, enc_value_back)
+    xs = [
+        flatten_rows(array)
+        for array in (
+            activated_low,
+            crossed_low,
+            cross_context_low,
+            normed_low,
+            context_low,
+            hidden,
+            encoder,
+        )
+    ]
+    gs = [
+        flatten_rows(array)
+        for array in (
+            down_low,
+            upward_low,
+            cross_res_low,
+            cross_query_back,
+            attn_low,
+            query_back,
+            key_back,
+            value_back,
+            rel_back,
+            enc_key_back,
+            enc_value_back,
+        )
+    ]
+    pairs = [(0, 0), (1, 1), (2, 2), (3, 3), (4, 4), (5, 5), (5, 6), (5, 7), (5, 8), (6, 9), (6, 10)]
+    gain_parts = jnp.stack([gainattn_part, gaincross_part, gainffn_part])
+    if kernels:
+        gain_parts = jnp.transpose(gain_parts.reshape(3, devices, -1), (1, 0, 2))
+        gain_parts = jnp.pad(gain_parts, ((0, 0), (0, 5), (0, 128 - gain_parts.shape[2])))
+        gain_parts = gain_parts.reshape(2, 2, ndp // 2, 2, 8, 128)
+        *sums, gain_sums = reduce_grads(xs, gs, pairs, gain_parts, ndp // 2)
+        gain_sums = gain_sums[:3, : width // devices]
+    else:
+        sums = [
+            lax.psum_scatter(
+                weight_grad(xs[i], gs[j]), ("seq", "dp"), scatter_dimension=0, tiled=True
+            )
+            for i, j in pairs
+        ]
+        gain_sums = lax.psum_scatter(gain_parts, ("seq", "dp"), scatter_dimension=1, tiled=True)
+    gainattn_sum, gaincross_sum, gainffn_sum = gain_sums
     (
+        down_sum,
+        up_sum,
+        cout_sum,
+        cquery_sum,
+        outproj_sum,
         query_sum,
         keyw_sum,
         valuew_sum,
-        outproj_sum,
         relative_sum,
-        cquery_sum,
         ckey_sum,
         cvalue_sum,
-        cout_sum,
-        up_sum,
-        down_sum,
-        gainattn_sum,
-        gaincross_sum,
-        gainffn_sum,
-    ) = (
-        lax.psum_scatter(query_part, ("seq", "dp"), scatter_dimension=0, tiled=True),
-        lax.psum_scatter(key_part, ("seq", "dp"), scatter_dimension=0, tiled=True),
-        lax.psum_scatter(value_part, ("seq", "dp"), scatter_dimension=0, tiled=True),
-        lax.psum_scatter(outproj_part, ("seq", "dp"), scatter_dimension=0, tiled=True),
-        lax.psum_scatter(relative_part, ("seq", "dp"), scatter_dimension=0, tiled=True),
-        lax.psum_scatter(crossquery_part, ("seq", "dp"), scatter_dimension=0, tiled=True),
-        lax.psum_scatter(crosskey_part, ("seq", "dp"), scatter_dimension=0, tiled=True),
-        lax.psum_scatter(crossvalue_part, ("seq", "dp"), scatter_dimension=0, tiled=True),
-        lax.psum_scatter(crossout_part, ("seq", "dp"), scatter_dimension=0, tiled=True),
-        lax.psum_scatter(up_part, ("seq", "dp"), scatter_dimension=0, tiled=True),
-        lax.psum_scatter(down_part, ("seq", "dp"), scatter_dimension=0, tiled=True),
-        lax.psum_scatter(gainattn_part, ("seq", "dp"), scatter_dimension=0, tiled=True),
-        lax.psum_scatter(gaincross_part, ("seq", "dp"), scatter_dimension=0, tiled=True),
-        lax.psum_scatter(gainffn_part, ("seq", "dp"), scatter_dimension=0, tiled=True),
-    )
+    ) = sums
     return (
         result.astype(jnp.bfloat16),
         hidden_grad,

time: 2430 us -> 760 us (0.31)
  waiting for transfers between devices: 1900 us -> 7.16 us
  Pallas kernels: 0 us -> 319 us
  blocking collectives: 68.2 us -> 0 us
  matrix products: 193 us -> 147 us
    reduce_scatter x5 -> x0, waiting for transfers between devices: 801 us -> none  [the longest x1 187 us: local(): lax.psum_scatter(up_part, ('seq', 'dp'), scatter_dimension=0, tiled=True)]
    unnamed x40 -> x12, waiting for transfers between devices: 727 us -> 0.16 us
    pallas_call x0 -> x2, Pallas kernels: none -> 319 us  [the longest x1 173 us: reduce_grads(): pl.pallas_call(lambda *refs: reduce_grads_kernel(plan, nz, len(xs), len(g...]
    all_gather x11 -> x0, waiting for transfers between devices: 288 us -> none  [the longest x1 77.9 us: local(): lax.all_gather(w_up, 'dp', axis=0, tiled=True)]
    dot_general x11 -> x0, matrix products: 58.8 us -> none  [weight_grad(): jnp.einsum('nd,ne->de', flatten_rows(array), flatten_rows(grad_rows), pre...]
    unnamed x1 -> x0, blocking collectives: 39.2 us -> none
    unnamed x285 -> x206, local copies, waits for them, and re-layouts: 98.9 us -> 66.4 us
    all_gather x3 -> x0, blocking collectives: 28.9 us -> none  [the longest x1 10.2 us: local(): lax.all_gather(gain_attn, 'dp', axis=0, tiled=True)]
  transfers between devices with their start and end apart: 30 -> 8, of which waited for: 25 -> 1; matrix products, arithmetic and copies ran while one was open for 13% -> 33% of each run, Pallas kernels for 0% -> 0%
where the time goes in v1:
time: 760 us; the launch traced here: 751 us
  Pallas kernels  319 us (42%)
  local copies, waits for them, and re-layouts  182 us (24%)
  matrix products  147 us (19%)
  other arithmetic  80 us (11%)
  between operations  15.6 us (2%)
    pallas_call x1, Pallas kernels, reduce_grads(): pl.pallas_call(lambda *refs: reduce_grads_kernel(plan, nz, len(xs), len(g...  173 us
    pallas_call x1, Pallas kernels, gather_weights(): pl.pallas_call(lambda *refs: gather_weights_kernel(count, nz, *refs), out...  146 us
    unnamed x206, local copies, waits for them, and re-layouts  66.4 us
    dot_general x11, matrix products, project_back(): jnp.einsum('ne,de->nd', flatten_rows(grad_rows), weight, preferred_elemen...  45.8 us
    dot_general x11, matrix products, project(): jnp.dot(flatten_rows(array), weight, preferred_element_type=jnp.float32)  35.1 us
    convert_element_type x1, other arithmetic, local(): activated_low = activated.astype(jnp.bfloat16)  15.2 us
  transfers between devices with their start and end apart: 8, of which 1 were waited for; matrix products, arithmetic and copies ran while one was open for 33% of the time, Pallas kernels for 0%

profile of v1, /device:TPU:0, one launch (start us, length us, event | category | flops | bytes accessed | tf_op | source)
XLA Modules:
  0.0 751.3 jit_solution(415424044323150270)
XLA Ops:
  8.5 146.2 %gather_weights.1 = (bf16[8,128,1024]{2,1,0:T(8,128)(2,1)}, bf16[8,128,1024]{2,1,0:T(8,128)(2,1)}, bf16[8,128,1024]{2,1,0:T(8,128)(2,1)}, bf16[8,128,512]{2,1,0:...) custom-call(bf16[128,1024]{1,0:T(8,128)(2,1)} %refs_0_.1, ...), custom_call_target="tpu_custom_call" | custom-call | tf_op jit(solution)/shard_map/gather_weights/pallas_call | solution.py:229
  175.2 4.7 fusion.40
  199.7 5.0 fusion.25
  207.0 8.4 %fusion.75 = (f32[3,2,16,64]{3,0,2,1:T(4,128)S(1)}, f32[3,2,16,64,256]{4,3,0,2,1:T(8,128)S(1)}) fusion(f32[64,256,3,2,16]{1,4,3,2,0:T(8,128)} %fusion.25, bf16[2,256,16,64,1]{1,3,4,2,0:T(8,128)(2,1)S(1)} %bitcast.438, bf16[3,2,64,16,64]{2,1,0,4,3:T(2,128)(2,1)S(1)} %convert_element_type.295, pred[3,2,64,256]{3,2,0,1:T(8,128)(4,1)S(1)} %broadcast_and_fusion), kind=kOutput, calls=%fused_computation.206 | convolution fusion | flops 206039040 | bytes 14540800 | tf_op jit(solution)/shard_map/jrthe,rshe->jrhts/dot_general | solution.py:513
  219.0 5.4 convert_reduce_fusion
  259.8 5.6 convert_reduce_fusion.1
  265.4 7.0 all-gather.9.cloned.1.call-done
  274.6 4.7 fusion.35
  290.0 8.6 %fusion.33 = (u8[2,64,4096]{2,1,0:T(8,128)(4,1)S(1)}, u8[2,64,4096]{2,1,0:T(8,128)(4,1)S(1)}, f32[3,2,64,4096]{3,2,1,0:T(8,128)S(1)}) fusion(bf16[3,2,64,1024]{3,2,1,0:T(8,128)(2,1)S(1)} %multiply_convert_fusion.4, bf16[1024,4096,1,1]{1,0,3,2:T(8,128)(2,1)} %bitcast.501), kind=kOutput, calls=%fused_computation.97 | convolution fusion | flops 3240624128 | bytes 16515072 | tf_op jit(solution)/shard_map/dot_general | solution.py:72
  298.6 15.2 %multiply_convert_fusion = (bf16[3,2,64,4096]{3,2,1,0:T(8,128)(2,1)S(1)}, f32[3,2,64,4096]{3,2,1,0:T(8,128)}) fusion(f32[3,2,64,4096]{3,2,1,0:T(8,128)S(1)} %get-tuple-element.111, u8[2,64,4096]{2,1,0:T(8,128)(4,1)S(1)} %get-tuple-element.66, u8[2,64,4096]{2,1,0:T(8,128)(4,1)S(1)} %get-tuple-element.65), kind=kLoop, calls=%fused_computation.30 | loop fusion | flops 110100480 | bytes 16777216 | tf_op jit(solution)/shard_map/convert_element_type | solution.py:556
  321.0 14.5 %add_convert_fusion = bf16[3,2,64,4096]{3,2,1,0:T(8,128)(2,1)} fusion(f32[3,2,64,4096]{3,2,1,0:T(8,128)} %get-tuple-element.88, f32[3,2,64,4096]{3,2,1,0:T(8,128)} %copy-done.17, bf16[3,2,64,1024]{3,2,1,0:T(8,128)(2,1)S(1)} %get-tuple-element.91, bf16[4096,1024,1,1]{1,0,3,2:T(8,128)(2,1)} %bitcast.503), kind=kOutput, calls=%fused_computation.29 | convolution fusion | flops 3243245568 | bytes 24903680 | tf_op jit(solution)/shard_map/ne,de->nd/dot_general | solution.py:77
  335.5 9.0 %multiply_reduce_fusion.1 = (f32[1024]{0:T(1024)}, f32[3,2,64]{2,1,0:T(2,128)S(1)}, f32[3,2,64,1024]{3,2,1,0:T(8,128)S(1)}) fusion(f32[3,2,64,1024]{3,2,1,0:T(8,128)S(1)} %get-tuple-element.110, f32[3,2,64]{2,1,0:T(2,128)S(1)} %fusion.62, f32[3,2,64]{2,1,0:T(2,128)S(1)} %broadcast_multiply_fusion.1, f32[1024]{0:T(1024)S(1)} %bitcast.496, ...), kind=kOutput, calls=%fused_computation.83 | convolution fusion | flops 3227515392 | bytes 17062400 | tf_op jit(solution)/shard_map/ne,de->nd/dot_general | solution.py:77
  359.9 6.0 fusion.8
  366.1 4.4 fusion.71
  382.4 5.9 multiply_reduce_fusion.2
  388.3 4.8 copy.324
  410.6 6.1 fusion.38
  416.7 4.7 copy.322
  425.6 9.0 %fusion.4 = (f32[3,2,16,64]{3,0,2,1:T(4,128)S(1)}, f32[2,16,256,3,64]{2,4,3,1,0:T(8,128)}) fusion(f32[3,2,16,64,256]{4,3,0,2,1:T(8,128)} %copy-done, f32[3,2,16,64]{3,0,2,1:T(4,128)} %get-tuple-element.77, f32[3,2,16,64]{3,0,2,1:T(4,128)S(1)} %bitcast_maximum_fusion, bf16[2,256,16,64,1]{1,3,4,2,0:T(8,128)(2,1)} %bitcast.441, ...), kind=kOutput, calls=%fused_computation.12 | convolution fusion | flops 207611904 | bytes 14491648 | tf_op jit(solution)/shard_map/jrthe,rshe->jrhts/dot_general | solution.py:586
  441.5 7.7 %fusion.68 = f32[3,2,16,64]{3,0,2,1:T(4,128)S(1)} fusion(f32[3,2,16,64,256]{4,3,0,2,1:T(8,128)} %copy-done, f32[3,2,16,64]{3,0,2,1:T(4,128)S(1)} %bitcast_maximum_fusion, f32[3,2,16,64]{3,0,2,1:T(4,128)S(1)} %negate_add_fusion, f32[3,2,16,64]{3,0,2,1:T(4,128)S(1)} %get-tuple-element.78, f32[2,16,256,3,64]{2,4,3,1,0:T(8,128)} %get-tuple-element.119), kind=kLoop, calls=%fused_computation.202 | loop fusion | flops 7858176 | bytes 12681216 | tf_op jit(solution)/shard_map/transpose(jvp())/reduce_sum | solution.py:51
  470.7 7.4 select_convert_fusion
  479.7 4.7 copy.318
  484.3 4.3 reshape.596
  552.8 172.5 %reduce_grads.1 = (f32[128,1024]{1,0:T(8,128)}, f32[32,4096]{1,0:T(8,128)}, f32[32,1024]{1,0:T(8,128)}, f32[32,1024]{1,0:T(8,128)}, f32[32,1024]{1,0:T(8,128)}, ...) custom-call(bf16[384,4096]{1,0:T(8,128)(2,1)} %bitcast.435, ...), custom_call_target="tpu_custom_call" | custom-call | tf_op jit(solution)/shard_map/reduce_grads/pallas_call | solution.py:408
  (364 shorter events, 264.0 us)
Async XLA Ops:
  7.2 197.7 %all-gather.7.cloned.1.call-start = ((), (), s32[]{:S(2)}) async-start(), calls=%async_computation.5 | async-start | bytes 1310720 | tf_op jit(solution)/shard_map/all_gather | solution.py:496
  8.5 146.2 %copy-start.48 = (bf16[3,2,64,1024]{3,2,1,0:T(8,128)(2,1)S(1)}, bf16[3,2,64,1024]{3,2,1,0:T(8,128)(2,1)}, u32[]{:S(2)}) copy-start(bf16[3,2,64,1024]{3,2,1,0:T(8,128)(2,1)} %param.20) | copy-start | bytes 2359300
  158.0 66.4 %all-gather.5.cloned.1.call-start = ((), (), s32[]{:S(2)}) async-start(), calls=%async_computation.4 | async-start | bytes 1310720 | tf_op jit(solution)/shard_map/all_gather | solution.py:497
  162.4 89.2 %all-gather.11.cloned.1.call-start = ((), (), s32[]{:S(2)}) async-start(), calls=%async_computation.7 | async-start | bytes 1310720 | tf_op jit(solution)/shard_map/all_gather | solution.py:498
  165.2 107.2 %all-gather.9.cloned.1.call-start = ((), (), s32[]{:S(2)}) async-start(), calls=%async_computation.6 | async-start | bytes 1310720 | tf_op jit(solution)/shard_map/all_gather | solution.py:499
  166.4 368.5 %reduce-scatter.19.cloned.1.call-start = ((), (), s32[]{:S(2)}) async-start(), calls=%async_computation.11 | async-start | bytes 1310720
  175.2 21.0 %copy-start.4 = (bf16[3,2,64,16,64]{4,3,2,1,0:T(8,128)(2,1)}, bf16[3,2,64,16,64]{4,3,2,1,0:T(8,128)(2,1)S(1)}, u32[]{:S(2)}) copy-start(bf16[3,2,64,16,64]{4,3,2,1,0:T(8,128)(2,1)S(1)} %convert_element_type.304) | copy-start | bytes 2359300
  183.2 23.8 %copy-start.2 = (bf16[3,2,64,16,64]{2,1,0,4,3:T(2,128)(2,1)}, bf16[3,2,64,16,64]{2,1,0,4,3:T(2,128)(2,1)S(1)}, u32[]{:S(2)}) copy-start(bf16[3,2,64,16,64]{2,1,0,4,3:T(2,128)(2,1)S(1)} %convert_element_type.295) | copy-start | bytes 2359300
  204.9 10.5 %copy-start.45 = (pred[3,2,64,256]{3,2,0,1:T(8,128)(4,1)}, pred[3,2,64,256]{3,2,0,1:T(8,128)(4,1)S(1)}, u32[]{:S(2)}) copy-start(pred[3,2,64,256]{3,2,0,1:T(8,128)(4,1)S(1)} %broadcast_and_fusion) | copy-start | bytes 294916
  207.0 8.4 %copy-start.10 = (bf16[2,256,1024]{1,2,0:T(8,128)(2,1)}, bf16[2,256,1024]{1,2,0:T(8,128)(2,1)S(1)}, u32[]{:S(2)}) copy-start(bf16[2,256,1024]{1,2,0:T(8,128)(2,1)S(1)} %copy.242) | copy-start | bytes 3145732
  289.4 24.5 %slice-start.2 = ((s8[8388608]{0:T(1024)(128)(4,1)}), s8[4194304]{0:T(1024)(128)(4,1)S(1)}, s32[]{:S(2)}) async-start(s8[8388608]{0:T(1024)(128)(4,1)} %bitcast.504), calls=%async_computation.14 | async-start | bytes 8388608
  290.0 8.6 %copy-start.22 = (bf16[3,2,64,1024]{3,2,1,0:T(8,128)(2,1)}, bf16[3,2,64,1024]{3,2,1,0:T(8,128)(2,1)S(1)}, u32[]{:S(2)}) copy-start(bf16[3,2,64,1024]{3,2,1,0:T(8,128)(2,1)S(1)} %multiply_convert_fusion.4) | copy-start | bytes 2359300
  290.0 23.9 %slice-start.3 = ((s8[8388608]{0:T(1024)(128)(4,1)}), s8[4194304]{0:T(1024)(128)(4,1)S(1)}, s32[]{:S(2)}) async-start(s8[8388608]{0:T(1024)(128)(4,1)} %bitcast.504), calls=%async_computation.15 | async-start | bytes 8388608
  298.6 15.2 %copy-start.17 = (f32[3,2,64,4096]{3,2,1,0:T(8,128)}, f32[3,2,64,4096]{3,2,1,0:T(8,128)S(1)}, u32[]{:S(2)}) copy-start(f32[3,2,64,4096]{3,2,1,0:T(8,128)S(1)} %get-tuple-element.111) | copy-start | bytes 18874372
  321.0 14.5 %copy-start.23 = (bf16[3,2,64,1024]{3,2,1,0:T(8,128)(2,1)}, bf16[3,2,64,1024]{3,2,1,0:T(8,128)(2,1)S(1)}, u32[]{:S(2)}) copy-start(bf16[3,2,64,1024]{3,2,1,0:T(8,128)(2,1)S(1)} %get-tuple-element.91) | copy-start | bytes 2359300
  355.8 10.2 %slice-start = ((s8[6291456]{0:T(1024)(128)(4,1)}), s8[4194304]{0:T(1024)(128)(4,1)S(1)}, s32[]{:S(2)}) async-start(s8[6291456]{0:T(1024)(128)(4,1)} %bitcast.433), calls=%async_computation.12 | async-start | bytes 8388608
  397.4 140.4 %reduce-scatter.17.cloned.1.call-start = ((), (), s32[]{:S(2)}) async-start(), calls=%async_computation.10 | async-start | bytes 1310720
  434.6 106.9 %reduce-scatter.15.cloned.1.call-start = ((), (), s32[]{:S(2)}) async-start(), calls=%async_computation.9 | async-start | bytes 1310720
  441.4 7.8 %copy-start.51 = (f32[3,2,16,64]{3,0,2,1:T(4,128)}, f32[3,2,16,64]{3,0,2,1:T(4,128)S(1)}, u32[]{:S(2)}) copy-start(f32[3,2,16,64]{3,0,2,1:T(4,128)S(1)} %negate_add_fusion) | copy-start | bytes 73732
  441.5 7.8 %copy-start.37 = (f32[3,2,16,64]{3,0,2,1:T(4,128)S(1)}, f32[3,2,16,64]{3,0,2,1:T(4,128)}, u32[]{:S(2)}) copy-start(f32[3,2,16,64]{3,0,2,1:T(4,128)} %copy-done.36) | copy-start | bytes 73732
  441.5 7.8 %copy-start.41 = (f32[3,2,16,64]{3,0,2,1:T(4,128)S(1)}, f32[3,2,16,64]{3,0,2,1:T(4,128)}, u32[]{:S(2)}) copy-start(f32[3,2,16,64]{3,0,2,1:T(4,128)} %copy.303) | copy-start | bytes 73732
  470.4 73.4 %reduce-scatter.13.cloned.1.call-start = ((), (), s32[]{:S(2)}) async-start(), calls=%async_computation.8 | async-start | bytes 1310720
  470.7 7.4 copy-start.3
  734.4 7.6 %copy-start.64 = (f32[32,1024]{1,0:T(8,128)S(1)}, f32[32,1024]{1,0:T(8,128)}, u32[]{:S(2)}) copy-start(f32[32,1024]{1,0:T(8,128)} %get-tuple-element.148) | copy-start | bytes 393220
  (73 other events, 271.7 us)
Sparse Core Ops, SparseCore 0:
  158.2 27.0 all-gather.6
  187.7 26.6 all-gather.4
  216.8 26.6 all-gather.10
  245.7 26.6 all-gather.8
  397.5 27.7 reduce-scatter.18
  434.7 27.7 reduce-scatter.16
  470.5 27.8 reduce-scatter.14
  501.6 27.7 reduce-scatter.12

commit v2 on v1

v2 whole, which is shorter than its diff:
```python
import math

import jax
import jax.numpy as jnp
from jax import lax
from jax.experimental import pallas as pl
from jax.experimental.pallas import tpu as pltpu
from jax.sharding import PartitionSpec as P

MESH = pl.DeviceIdType.MESH

HEADS = 16
HEAD_DIM = 64
BUCKETS = 32


eps_norm = 1e-05
bucket_edges = [step_index for step_index in range(1, 16)] + [
    int(math.ceil(16 * 8 ** ((step_index - 16) / 16))) for step_index in range(16, 32)
]


def flatten_rows(array):
    return array.reshape(-1, array.shape[-1])


def weight_grad(array, grad_rows):
    return jnp.einsum(
        "nd,ne->de",
        flatten_rows(array),
        flatten_rows(grad_rows),
        preferred_element_type=jnp.float32,
    )


def remote(src, dst, send, recv, to):
    return pltpu.make_async_remote_copy(
        src_ref=src, dst_ref=dst, send_sem=send, recv_sem=recv, device_id=to, device_id_type=MESH
    )


def place():
    s = lax.axis_index("seq")
    d = lax.axis_index("dp")
    z, c = d // 2, lax.rem(d, 2)
    sx = s + 1 - 2 * lax.rem(s, 2)
    sy = lax.rem(s + 2, 4)
    return s, z, c, sx, sy


def greet(nz):
    s, z, c, sx, sy = place()
    barrier = pltpu.get_barrier_semaphore()
    dests = [(s, 2 * z + 1 - c), (sx, 2 * z + c), (sy, 2 * z + c)]
    for dz in range(1, nz):
        dests.append((s, 2 * lax.rem(z + dz, nz) + c))
    for dest in dests:
        pl.semaphore_signal(barrier, inc=1, device_id=dest, device_id_type=MESH)
    pl.semaphore_wait(barrier, len(dests))


def gather_weights_kernel(count, nz, *refs):
    shards, planes = refs[:count], refs[count : count + 2]
    wholes, full_planes = refs[count + 2 : 2 * count + 2], refs[2 * count + 2 : 2 * count + 4]
    local_sem, send, recv, plane_send, plane_recv = refs[2 * count + 4 :]
    s, z, c, sx, sy = place()
    own = 2 * z + c
    core = (s, 2 * z + 1 - c)
    beside_x, beside_y = (sx, own), (sy, own)
    greet(nz)
    started = []

    def put(copy):
        copy.start()
        started.append(copy)

    items = []
    for w in range(count):
        if shards[w].shape[0] % 128:
            items.append((w, 0, 0, None))
            continue
        for row in range(0, shards[w].shape[0], 128):
            wide = min(shards[w].shape[1], 1024)
            for col in range(0, shards[w].shape[1], wide):
                items.append((w, row, 128, pl.ds(col, wide)))
    steps = len(items)
    split = [item[2] > 0 for item in items]

    def cut(ref, i, q=None, half=None):
        _, row, height, cols = items[i]
        if not height:
            return ref
        if q is not None:
            height = height // 4
            row = row + q * height
        if half is not None:
            height = height // 2
            row = row + half * height
        return ref.at[pl.ds(row, height), cols]

    def shard(i, q=None):
        return cut(shards[items[i][0]], i, q)

    def whole(i, block, q=None, half=None):
        return cut(wholes[items[i][0]].at[block], i, q, half)

    def along_z(i):
        here = pltpu.make_async_copy(shard(i), whole(i, own), local_sem.at[i])
        here.start()
        started.append(here)
        q = s if split[i] else None
        for dz in range(1, nz):
            to = (s, 2 * lax.rem(z + dz, nz) + c)
            put(remote(shard(i, q), whole(i, own, q), send.at[i, dz, 0], recv.at[i, dz, 0], to))
        put(remote(shard(i), whole(i, own), send.at[i, 0, 0], recv.at[i, 0, 0], core))

    def moved(i, dz, kind, q, half, to):
        part = whole(i, 2 * lax.rem(z + nz - dz, nz) + c, q if split[i] else None, half)
        return remote(part, part, send.at[i, dz, kind], recv.at[i, dz, kind], to)

    def to_core(i, dz, kind, q, half):
        put(moved(i, dz, kind, q, half, core))

    def first(i):
        for dz in range(1, nz):
            moved(i, dz, 0, s, None, core).wait_recv()
            if split[i]:
                put(moved(i, dz, 1, s, None, beside_x))
                put(moved(i, dz, 2, s, None, beside_y))
            to_core(i, dz, 5, s, None)

    def second(i):
        if not split[i]:
            return
        for dz in range(1, nz):
            moved(i, dz, 1, sx, None, core).wait_recv()
            put(moved(i, dz, 4, sx, 0, beside_y))
            to_core(i, dz, 6, sx, None)
            moved(i, dz, 2, sy, None, core).wait_recv()
            put(moved(i, dz, 3, sy, 1, beside_x))
            to_core(i, dz, 7, sy, None)

    def third(i):
        if not split[i]:
            return
        for dz in range(1, nz):
            moved(i, dz, 4, 3 - s, 0, core).wait_recv()
            to_core(i, dz, 8, 3 - s, 0)
            moved(i, dz, 3, 3 - s, 1, core).wait_recv()
            to_core(i, dz, 9, 3 - s, 1)

    def last(i):
        other = 1 - c
        block = whole(i, 2 * z + other)
        remote(block, block, send.at[i, 0, 0], recv.at[i, 0, 0], core).wait_recv()
        for dz in range(1, nz):
            kinds = [(5, s if split[i] else None, None)]
            if split[i]:
                kinds += [(6, sx, None), (7, sy, None), (8, 3 - s, 0), (9, 3 - s, 1)]
            for kind, q, half in kinds:
                part = whole(i, 2 * lax.rem(z + nz - dz, nz) + other, q, half)
                remote(part, part, send.at[i, dz, kind], recv.at[i, dz, kind], core).wait_recv()

    def plane(i, kind, q, half, to):
        rows = full_planes[i].shape[0]
        part = full_planes[i].at[pl.ds(half * (rows // 2), rows // 2), q]
        return remote(part, part, plane_send.at[i, kind], plane_recv.at[i, kind], to)

    def plane_part(i):
        return planes[i].at[0] if len(planes[i].shape) == 4 else planes[i]

    def plane_whole(i, kind, q, to):
        return remote(
            plane_part(i), full_planes[i].at[:, q], plane_send.at[i, kind], plane_recv.at[i, kind], to
        )

    def plane_first(i):
        here = pltpu.make_async_copy(plane_part(i), full_planes[i].at[:, s], local_sem.at[steps + i])
        here.start()
        started.append(here)
        put(plane_whole(i, 0, s, beside_x))
        put(plane_whole(i, 1, s, beside_y))

    def plane_second(i):
        plane_whole(i, 0, sx, core).wait_recv()
        put(plane(i, 2, sx, 0, beside_y))
        plane_whole(i, 1, sy, core).wait_recv()
        put(plane(i, 3, sy, 1, beside_x))

    def plane_last(i):
        plane(i, 2, 3 - s, 0, core).wait_recv()
        plane(i, 3, 3 - s, 1, core).wait_recv()

    ahead = 4
    for i in range(2):
        plane_first(i)
    for i in range(min(ahead, steps)):
        along_z(i)
    for i in range(steps + 2):
        if i < steps:
            first(i)
        if ahead + i < steps:
            along_z(ahead + i)
        if 1 <= i <= steps:
            second(i - 1)
        if i in (1, 2):
            plane_second(i - 1)
        if i >= 2:
            third(i - 2)
    for i in range(2):
        plane_last(i)
    for i in range(steps):
        last(i)
    for copy in started:
        if hasattr(copy, "wait_send") and copy.is_remote:
            copy.wait_send()
        else:
            copy.wait()


def gather_weights(shards, hidden, encoder, ndp):
    nz = ndp // 2
    count = len(shards)
    steps = sum(max(1, w.size // (128 * 1024)) for w in shards)
    planes = jax.ShapeDtypeStruct((encoder.shape[0], 4) + encoder.shape[1:], encoder.dtype)
    return pl.pallas_call(
        lambda *refs: gather_weights_kernel(count, nz, *refs),
        out_shape=[jax.ShapeDtypeStruct((ndp,) + w.shape, w.dtype) for w in shards] + [planes] * 2,
        in_specs=[pl.BlockSpec(memory_space=pltpu.VMEM)] * (count + 2),
        out_specs=[pl.BlockSpec(memory_space=pl.ANY)] * (count + 2),
        scratch_shapes=[
            pltpu.SemaphoreType.DMA((steps + 2,)),
            pltpu.SemaphoreType.DMA((steps, nz, 10)),
            pltpu.SemaphoreType.DMA((steps, nz, 10)),
            pltpu.SemaphoreType.DMA((2, 4)),
            pltpu.SemaphoreType.DMA((2, 4)),
        ],
        compiler_params=pltpu.CompilerParams(collective_id=0, has_side_effects=True),
        name="gather_weights",
    )(*shards, hidden, encoder)


RING = 8


def reduce_grads_kernel(plan, nz, n_x, n_g, n_out, *refs):
    at = 0
    xs, at = refs[at : at + n_x], at + n_x
    gs, at = refs[at : at + n_g], at + n_g
    gain_part, at = refs[at], at + 1
    shares, at = refs[at : at + 2], at + 2
    outs, at = refs[at : at + n_out], at + n_out
    gain_out, at = refs[at], at + 1
    share_outs, at = refs[at : at + 2], at + 2
    kinds = []
    for _ in range(3):
        kinds.append(refs[at : at + 5])
        at += 5
    share1, share2, send, recv, credit = refs[at:]
    s, z, c, sx, sy = place()
    own = 2 * z + c
    x, y = lax.rem(s, 2), s // 2
    core = (s, 2 * z + 1 - c)
    beside_x, beside_y = (sx, own), (sy, own)
    greet(nz)
    count = len(plan)

    def buffers(k):
        kind, slot = plan[k][0], plan[k][1]
        if kind == 3:
            return None, shares[slot // 2].at[:, :, slot % 2], share1.at[slot], share2.at[slot], None
        part, held0, held1, held2, held3 = kinds[kind]
        if kind == 2:
            return gain_part, held0.at[slot], held1.at[slot], held2.at[slot], held3.at[slot]
        return (part.at[slot % 2], held0.at[slot % RING], held1.at[slot], held2.at[slot], held3.at[slot])

    def core_copy(k):
        part, held0 = buffers(k)[:2]
        return remote(part.at[:, :, :, 1 - c], held0, send.at[k, 0], recv.at[k, 0], core)

    def first_copy(k):
        _, held0, held1 = buffers(k)[:3]
        if k % 2 == 0:
            return remote(held0.at[:, 1 - x], held1, send.at[k, 1], recv.at[k, 1], beside_x)
        return remote(held0.at[1 - y], held1, send.at[k, 1], recv.at[k, 1], beside_y)

    def second_copy(k):
        held1, held2 = buffers(k)[2:4]
        if k % 2 == 0:
            return remote(held1.at[1 - y], held2, send.at[k, 2], recv.at[k, 2], beside_y)
        return remote(held1.at[1 - x], held2, send.at[k, 2], recv.at[k, 2], beside_x)

    def z_copy(k, dz):
        held2, held3 = buffers(k)[3:5]
        zt = lax.rem(z + dz, nz)
        return remote(
            held2.at[zt], held3.at[dz - 1], send.at[k, 2 + dz], recv.at[k, 2 + dz], (s, 2 * zt + c)
        )

    def added(held, mine):
        held[...] = (held[...].astype(jnp.float32) + mine.astype(jnp.float32)).astype(held.dtype)

    def make(k):
        kind, slot, xi, gi, _, col, wide = plan[k]
        if kind == 3:
            return
        if kind < 2:
            part = buffers(k)[0]
            left, right = xs[xi], gs[gi]
            block = part.shape[4]
            if slot >= 2:
                core_copy(before[k]).wait_send()
            group = 256 // block
            for i in range(left.shape[1] // 256):
                product = lax.dot_general(
                    left[:, i * 256 : (i + 1) * 256],
                    right[:, col : col + wide],
                    (((0,), (0,)), ((), ())),
                    preferred_element_type=jnp.float32,
                )
                index = i * group
                i_s, rest = divmod(index, 2 * nz)
                zs = rest // 2
                part[i_s // 2, i_s % 2, zs : zs + group // 2] = product.reshape(group // 2, 2, block, wide).astype(
                    part.dtype
                )
        if kind < 2 and slot >= RING:
            pl.semaphore_wait(credit.at[kind], 1)
        core_copy(k).start()

    def after_core(k):
        part, held0 = buffers(k)[:2]
        if plan[k][0] == 3:
            first_copy(k).start()
            return
        core_copy(k).wait_recv()
        added(held0, part[:, :, :, c])
        first_copy(k).start()

    def after_first(k):
        _, held0, held1 = buffers(k)[:3]
        first_copy(k).wait_recv()
        added(held1, held0[:, x] if k % 2 == 0 else held0[y])
        second_copy(k).start()
        kind, slot = plan[k][:2]
        first_copy(k).wait_send()
        if kind < 2 and slot + RING < sum(p[0] == kind for p in plan):
            pl.semaphore_signal(credit.at[kind], inc=1, device_id=core, device_id_type=MESH)

    def after_second(k):
        held1, held2 = buffers(k)[2:4]
        second_copy(k).wait_recv()
        if plan[k][0] == 3:
            mine = (held1[y] if k % 2 == 0 else held1[x]).astype(jnp.float32)
            slot = plan[k][1]
            share_outs[slot // 2][slot % 2] = held2[...].astype(jnp.float32) + mine
            return
        added(held2, held1[y] if k % 2 == 0 else held1[x])
        for dz in range(1, nz):
            z_copy(k, dz).start()

    def finish(k):
        if plan[k][0] == 3:
            return
        held2, held3 = buffers(k)[3:5]
        total = held2[z].astype(jnp.float32)
        for dz in range(1, nz):
            z_copy(k, dz).wait_recv()
            total = total + held3[dz - 1].astype(jnp.float32)
        kind, _, _, _, oi, col, wide = plan[k]
        if kind == 2:
            gain_out[...] = total
        else:
            outs[oi][:, col : col + wide] = total

    before = {}
    recent = {}
    for k in range(count):
        kind, slot = plan[k][0], plan[k][1]
        before[k] = recent.get((kind, slot - 2))
        recent[(kind, slot)] = k
    followed = set(v for v in before.values() if v is not None)

    for t in range(count + 7):
        if t >= 7:
            finish(t - 7)
        if 5 <= t < count + 5:
            after_second(t - 5)
        if 3 <= t < count + 3:
            after_first(t - 3)
        if t < count:
            make(t)
        if 1 <= t < count + 1:
            after_core(t - 1)
    for k in range(count):
        if k not in followed and plan[k][0] < 3:
            core_copy(k).wait_send()
        second_copy(k).wait_send()
        for dz in range(1, nz if plan[k][0] < 3 else 1):
            z_copy(k, dz).wait_send()


def reduce_grads(xs, gs, pairs, gain_part, shares, nz):
    plan, slots = [(3, i, 0, 0, 0, 0, 0) for i in range(4)], [0, 0, 0]
    blocks, columns = [], []
    ndev = 8 * nz
    for oi, (xi, gi) in enumerate(pairs):
        rows, wide = xs[xi].shape[1], gs[gi].shape[1]
        columns.append((rows // ndev, wide))
        kind = 0 if rows // ndev <= 32 else 1
        step = (512, 256)[kind]
        for col in range(0, wide, step):
            plan.append((kind, slots[kind], xi, gi, oi, col, step))
            slots[kind] += 1
    plan.append((2, 0, 0, 0, 0, 0, 128))
    rb = min(rows for rows, _ in columns)
    shapes = [((rb, 512), jnp.bfloat16, slots[0]), ((max(rows for rows, _ in columns), 256), jnp.bfloat16, slots[1])]
    scratch = []
    for (tail, kind_type, n) in shapes + [((8, 128), jnp.float32, 1)]:
        scratch.append(
            pltpu.VMEM((2, 2, 2, nz, 2) + tail if kind_type == jnp.bfloat16 else (8, 128), kind_type)
        )
        scratch.append(pltpu.VMEM((min(n, RING), 2, 2, nz) + tail, kind_type))
        scratch.append(pltpu.VMEM((n, 2, nz) + tail, kind_type))
        scratch.append(pltpu.VMEM((n, nz) + tail, kind_type))
        scratch.append(pltpu.VMEM((n, nz - 1) + tail, kind_type))
    n = len(plan)
    vmem = pl.BlockSpec(memory_space=pltpu.VMEM)
    outs = [jax.ShapeDtypeStruct(shape, jnp.float32) for shape in columns]
    outs.append(jax.ShapeDtypeStruct((8, 128), jnp.float32))
    share = shares[0].shape[3:]
    outs += [jax.ShapeDtypeStruct(a.shape[2:], jnp.float32) for a in shares]
    return pl.pallas_call(
        lambda *refs: reduce_grads_kernel(plan, nz, len(xs), len(gs), len(columns), *refs),
        out_shape=outs,
        in_specs=[vmem] * (len(xs) + len(gs) + 3),
        out_specs=[vmem] * len(outs),
        scratch_shapes=scratch
        + [pltpu.VMEM((4, 2) + share, jnp.bfloat16), pltpu.VMEM((4,) + share, jnp.bfloat16)]
        + [pltpu.SemaphoreType.DMA((n, 2 + nz)), pltpu.SemaphoreType.DMA((n, 2 + nz))]
        + [pltpu.SemaphoreType.REGULAR((2,))],
        compiler_params=pltpu.CompilerParams(
            collective_id=1, has_side_effects=True, vmem_limit_bytes=62 * 2**20
        ),
        name="reduce_grads",
    )(*xs, *gs, gain_part, *shares)

NEG = -1000000000.0


def mm(left, right):
    return jnp.dot(left, right, preferred_element_type=jnp.float32)


def mm_back(left, right):
    return lax.dot_general(
        left, right, (((1,), (1,)), ((), ())), preferred_element_type=jnp.float32
    )


def mm_grad(left, right):
    return lax.dot_general(
        left, right, (((0,), (0,)), ((), ())), preferred_element_type=jnp.float32
    )


def tiles(width, body):
    def step(i, carry):
        body(pl.ds(pl.multiple_of(i * 256, 256), 256))
        return carry

    lax.fori_loop(0, width // 256, step, 0)


def row_tiles(rows, body, step_rows=64):
    def step(i, carry):
        body(pl.ds(pl.multiple_of(i * step_rows, step_rows), step_rows))
        return carry

    lax.fori_loop(0, rows // step_rows, step, 0)


def heads_in(tile):
    lane = lax.broadcasted_iota(jnp.int32, tile.shape, 1) // (tile.shape[1] // 4)
    return jnp.concatenate(
        [jnp.where(lane == h, tile, jnp.zeros_like(tile)) for h in range(4)], axis=0
    )


def heads_out(stacked):
    n, wide = stacked.shape[0] // 4, stacked.shape[1]
    lane = lax.broadcasted_iota(jnp.int32, (n, wide), 1) // (wide // 4)
    result = stacked[3 * n :]
    for h in (2, 1, 0):
        result = jnp.where(lane == h, stacked[h * n : (h + 1) * n], result)
    return result


def head_lanes(columns, wide):
    n = columns[0].shape[0]
    lane = lax.broadcasted_iota(jnp.int32, (n, wide), 1) // (wide // 4)
    result = jnp.broadcast_to(columns[3], (n, wide))
    for h in (2, 1, 0):
        result = jnp.where(lane == h, jnp.broadcast_to(columns[h], (n, wide)), result)
    return result


def head_sums(product):
    n, wide = product.shape
    lane = lax.broadcasted_iota(jnp.int32, (n, wide), 1) // (wide // 4)
    return [
        jnp.sum(jnp.where(lane == h, product, 0.0), axis=1, keepdims=True) for h in range(4)
    ]


def bucket_of(distance):
    total = jnp.zeros_like(distance)
    for edge in bucket_edges:
        total = total + (distance >= edge).astype(jnp.int32)
    return total


def hot_forward(start, span):
    lag = lax.broadcasted_iota(jnp.int32, (128, span), 1)
    row = lax.rem(lax.broadcasted_iota(jnp.int32, (128, span), 0), BUCKETS)
    distance = lax.rem(start - lag + span, span)
    return jnp.where(bucket_of(distance) == row, 1.0, 0.0).astype(jnp.bfloat16)


def hot_backward(start, span):
    lag = lax.broadcasted_iota(jnp.int32, (span, 128), 0)
    column = lax.rem(lax.broadcasted_iota(jnp.int32, (span, 128), 1), BUCKETS)
    distance = lax.rem(start + lag + 1, span)
    return jnp.where(bucket_of(distance) == column, 1.0, 0.0).astype(jnp.bfloat16)


def skewed(array, block):
    return jnp.concatenate(
        [
            pltpu.roll(array[i : i + block], 0, 1, stride=1, stride_axis=0)
            for i in range(0, array.shape[0], block)
        ],
        axis=0,
    )


def norm_rows(values):
    centred = values - jnp.mean(values, axis=1, keepdims=True)
    scale = lax.rsqrt(jnp.mean(centred * centred, axis=1, keepdims=True) + eps_norm)
    return centred * scale, scale


def norm_back(grad, normal, scale, gain):
    grad = grad * gain
    return scale * (
        grad
        - jnp.mean(grad, axis=1, keepdims=True)
        - normal * jnp.mean(grad * normal, axis=1, keepdims=True)
    )


def add_rows(total_ref, index, product):
    total_ref[index] += jnp.sum(product.reshape(-1, 8, product.shape[1]), axis=0)


class Fetch:
    def __init__(self, sources, targets, sems):
        self.copies = [
            pltpu.make_async_copy(src, dst, sems.at[i])
            for i, (src, dst) in enumerate(zip(sources, targets))
        ]
        self.targets = targets
        self.waited = set()
        for copy in self.copies:
            copy.start()

    def __getitem__(self, i):
        if i not in self.waited:
            self.waited.add(i)
            self.copies[i].wait()
        return self.targets[i]


def forward_kernel(rows, local_len, *refs):
    (
        hidden,
        mains,
        states,
        lengths,
        enc_lengths,
        gains,
        *weights,
    ) = refs[:14]
    (hid, x_all, query, keys, values, prob, prob_own, context, ckeys, cvalues) = refs[14:24]
    (normal, normal_scale, normed_low, cquery, cprob, ccontext) = refs[24:30]
    rel, residual = refs[30:32]
    fetch = Fetch(weights, refs[32:40], refs[40])
    w_key, w_value, w_query, w_relative, w_ckey, w_cvalue, w_out, w_cquery = range(8)
    width = hid.shape[1]
    mine = 3 * local_len
    span = mains.shape[0] // rows
    start = lax.axis_index("seq") * local_len
    x_all[: rows * span] = mains[...]
    for r in range(rows):
        for j in range(3):
            tile = hidden[j, r]
            hid[r * mine + j * local_len : r * mine + (j + 1) * local_len] = tile
            if j:
                at = rows * span + (2 * r + j - 1) * local_len
                x_all[at : at + local_len] = tile

    def project(left, w, target, scale=None):
        weight = fetch[w]

        def body(cols):
            product = mm(left[...], weight[:, cols])
            if scale is not None:
                product = product * scale
            target[:, cols] = product.astype(target.dtype)

        tiles(target.shape[1], body)

    project(x_all, w_key, keys)
    project(x_all, w_value, values)
    project(hid, w_query, query, 0.125)
    project(hid, w_relative, rel)
    hot = hot_forward(start, span)

    def attend(step, carry):
        r, g = step // 4, lax.rem(step, 4)
        cols = pl.ds(pl.multiple_of(g * 256, 256), 256)
        own_rows = pl.ds(pl.multiple_of(r * mine, local_len), mine)
        main_rows = pl.ds(pl.multiple_of(r * span, span), span)
        side_rows = pl.ds(pl.multiple_of(rows * span + r * 2 * local_len, local_len), 2 * local_len)
        q_tile = query[own_rows, cols]
        rel_tile = rel[own_rows, pl.ds(pl.multiple_of(g * 128, 128), 128)]
        side_key = keys[side_rows, cols].astype(jnp.float32)
        side_value = values[side_rows, cols].astype(jnp.float32)
        zero = jnp.zeros((local_len, 256), jnp.float32)
        scores = mm_back(heads_in(q_tile), keys[main_rows, cols])
        bias = skewed(mm(heads_in(rel_tile), hot), local_len)
        products = q_tile.astype(jnp.float32) * jnp.concatenate([zero, side_key], axis=0)
        own_dot = head_sums(products)
        rel_lane = lax.broadcasted_iota(jnp.int32, (mine, 128), 1)
        rel_wide = rel_tile.astype(jnp.float32)
        row = lax.broadcasted_iota(jnp.int32, (mine, span), 0)
        at = lax.broadcasted_iota(jnp.int32, (mine, span), 1)
        ahead = start + lax.rem(row, local_len) + jnp.where(row < local_len, 1, 0)
        kept = (at < ahead) & (at < lengths[r])
        first = lax.broadcasted_iota(jnp.int32, (mine, 1), 0) < local_len
        low, owns = [], []
        for h in range(4):
            part = slice(h * mine, (h + 1) * mine)
            score = jnp.where(kept, scores[part] + bias[part], NEG)
            near = jnp.sum(jnp.where(rel_lane == h * BUCKETS, rel_wide, 0.0), axis=1, keepdims=True)
            own = jnp.where(first, NEG, own_dot[h] + near)
            peak = jnp.maximum(jnp.max(score, axis=1, keepdims=True), own)
            power = jnp.exp(score - peak)
            own_power = jnp.exp(own - peak)
            share = 1.0 / (jnp.sum(power, axis=1, keepdims=True) + own_power)
            low.append((power * share).astype(jnp.bfloat16))
            owns.append(own_power * share)
        low = jnp.concatenate(low, axis=0)
        prob[step] = low
        spread = head_lanes(owns, 256)
        prob_own[own_rows, cols] = spread
        total = heads_out(mm(low, values[main_rows, cols]))
        total = total + spread * jnp.concatenate([zero, side_value], axis=0)
        context[own_rows, cols] = total.astype(context.dtype)
        return carry

    lax.fori_loop(0, 4 * rows, attend, 0)
    project(states, w_ckey, ckeys)
    project(states, w_cvalue, cvalues)
    weight_out = fetch[w_out]

    def out_body(cols):
        residual[:, cols] = hid[:, cols].astype(jnp.float32) + mm(context[...], weight_out[:, cols])

    tiles(width, out_body)

    def norm_body(part):
        normal[part], scale = norm_rows(residual[part])
        normal_scale[part] = jnp.broadcast_to(scale, (scale.shape[0], 128))
        normed_low[part] = (normal[part] * gains[0:1]).astype(jnp.bfloat16)

    row_tiles(hid.shape[0], norm_body)
    project(normed_low, w_cquery, cquery, 0.125)

    def cross(step, carry):
        r, g = step // 4, lax.rem(step, 4)
        cols = pl.ds(pl.multiple_of(g * 256, 256), 256)
        own_rows = pl.ds(pl.multiple_of(r * mine, local_len), mine)
        main_rows = pl.ds(pl.multiple_of(r * span, span), span)
        scores = mm_back(heads_in(cquery[own_rows, cols]), ckeys[main_rows, cols])
        at = lax.broadcasted_iota(jnp.int32, (mine, span), 1)
        kept = at < enc_lengths[r]
        low = []
        for h in range(4):
            score = jnp.where(kept, scores[h * mine : (h + 1) * mine], NEG)
            power = jnp.exp(score - jnp.max(score, axis=1, keepdims=True))
            share = 1.0 / jnp.sum(power, axis=1, keepdims=True)
            low.append((power * share).astype(jnp.bfloat16))
        low = jnp.concatenate(low, axis=0)
        cprob[step] = low
        ccontext[own_rows, cols] = heads_out(mm(low, cvalues[main_rows, cols])).astype(
            ccontext.dtype
        )
        return carry

    lax.fori_loop(0, 4 * rows, cross, 0)


def middle_kernel(
    rows,
    local_len,
    normal,
    ccontext,
    gains,
    cotangent,
    any_cout,
    any_up,
    any_down,
    output,
    crossed_low,
    activated,
    last_low,
    up_back,
    cross_grad,
    cross_low,
    ccontext_back,
    gain_total,
    normal2,
    scale2,
    slope,
    residual,
    v_cout,
    v_up,
    v_down,
    sems,
):
    fetch = Fetch((any_cout, any_up, any_down), (v_cout, v_up, v_down), sems)
    tokens, width = normal.shape
    mine = 3 * local_len
    gain_total[...] = jnp.zeros_like(gain_total)
    weight_cout = fetch[0]

    def cross_body(cols):
        residual[:, cols] = normal[:, cols] * gains[0:1, cols] + mm(
            ccontext[...], weight_cout[:, cols]
        )

    tiles(width, cross_body)

    def norm_body(part):
        normal2[part], scale = norm_rows(residual[part])
        scale2[part] = jnp.broadcast_to(scale, (scale.shape[0], 128))
        crossed_low[part] = (normal2[part] * gains[1:2]).astype(jnp.bfloat16)

    row_tiles(tokens, norm_body)
    weight_up = fetch[1]

    def up_body(cols):
        value = mm(crossed_low[...], weight_up[:, cols])
        below = 0.5 + 0.5 * lax.erf(value * (0.5**0.5))
        activated[:, cols] = (value * below).astype(jnp.bfloat16)
        density = jnp.exp(-0.5 * value * value) * (1.0 / math.sqrt(2.0 * math.pi))
        slope[:, cols] = (below + value * density).astype(jnp.bfloat16)

    tiles(activated.shape[1], up_body)
    weight_down = fetch[2]

    def down_body(cols):
        residual[:, cols] = normal2[:, cols] * gains[1:2, cols] + mm(
            activated[...], weight_down[:, cols]
        )

    tiles(width, down_body)
    for r in range(rows):
        for j in range(3):
            at = r * mine + j * local_len
            part = slice(at, at + local_len)
            normal3, scale = norm_rows(residual[part])
            output[j, r] = (normal3 * gains[2:3]).astype(output.dtype)
            above = cotangent[j, r].astype(jnp.float32)
            add_rows(gain_total, 2, above * normal3)
            grad = norm_back(above, normal3, scale, gains[2:3])
            residual[part] = grad
            last_low[part] = grad.astype(jnp.bfloat16)

    def down_back(cols):
        product = mm_back(last_low[...], weight_down[cols, :])
        up_back[:, cols] = (product * slope[:, cols].astype(jnp.float32)).astype(jnp.bfloat16)

    tiles(activated.shape[1], down_back)

    def up_back_body(cols):
        residual[:, cols] = residual[:, cols] + mm_back(up_back[...], weight_up[cols, :])

    tiles(width, up_back_body)

    def cross_norm_back(part):
        above = residual[part]
        add_rows(gain_total, 1, above * normal2[part])
        grad = norm_back(above, normal2[part], scale2[part][:, 0:1], gains[1:2])
        cross_grad[part] = grad
        cross_low[part] = grad.astype(jnp.bfloat16)

    row_tiles(tokens, cross_norm_back)

    def cout_back(cols):
        ccontext_back[:, cols] = mm_back(cross_low[...], weight_cout[cols, :]).astype(jnp.bfloat16)

    tiles(width, cout_back)


def backward_kernel(rows, local_len, *refs):
    (
        ccontext_back,
        cross_grad,
        cquery,
        ckeys,
        cvalues,
        cprob,
        normal,
        normal_scale,
        gains,
        query,
        keys,
        values,
        prob,
        prob_own,
        *weights,
    ) = refs[:22]
    (cquery_back, ckey_back, cvalue_back, attn_low, query_back, key_back) = refs[22:28]
    (value_back, rel_back, hidden_own, main_part, states_part, gain_total) = refs[28:34]
    residual, context_back = refs[34:36]
    fetch = Fetch(weights, refs[36:44], refs[44])
    w_cquery, w_out, w_ckey, w_cvalue, w_query, w_relative, w_key, w_value = range(8)
    tokens, width = query.shape
    mine = 3 * local_len
    span = ckeys.shape[0] // rows
    start = lax.axis_index("seq") * local_len
    gain_total[...] = jnp.zeros_like(gain_total)

    def cross(step, carry):
        r, g = step // 4, lax.rem(step, 4)
        cols = pl.ds(pl.multiple_of(g * 256, 256), 256)
        own_rows = pl.ds(pl.multiple_of(r * mine, local_len), mine)
        main_rows = pl.ds(pl.multiple_of(r * span, span), span)
        above = heads_in(ccontext_back[own_rows, cols])
        grads = mm_back(above, cvalues[main_rows, cols])
        low = []
        for h in range(4):
            part = slice(h * mine, (h + 1) * mine)
            share = cprob[step, part].astype(jnp.float32)
            weighted = share * grads[part]
            low.append(
                (weighted - share * jnp.sum(weighted, axis=1, keepdims=True)).astype(jnp.bfloat16)
            )
        low = jnp.concatenate(low, axis=0)
        back = heads_out(mm(low, ckeys[main_rows, cols])).astype(jnp.bfloat16)
        cquery_back[own_rows, cols] = back * jnp.bfloat16(0.125)
        ckey_back[main_rows, cols] = mm_grad(low, heads_in(cquery[own_rows, cols])).astype(
            jnp.bfloat16
        )
        cvalue_back[main_rows, cols] = mm_grad(cprob[step], above).astype(jnp.bfloat16)
        return carry

    lax.fori_loop(0, 4 * rows, cross, 0)
    weight_cquery = fetch[w_cquery]

    def cquery_body(cols):
        residual[:, cols] = cross_grad[:, cols] + mm_back(cquery_back[...], weight_cquery[cols, :])

    tiles(width, cquery_body)

    def attn_norm_back(part):
        above = residual[part]
        add_rows(gain_total, 0, above * normal[part])
        grad = norm_back(above, normal[part], normal_scale[part][:, 0:1], gains[0:1])
        residual[part] = grad
        attn_low[part] = grad.astype(jnp.bfloat16)

    row_tiles(tokens, attn_norm_back)
    weight_out = fetch[w_out]

    def out_back(cols):
        context_back[:, cols] = mm_back(attn_low[...], weight_out[cols, :]).astype(jnp.bfloat16)

    tiles(width, out_back)
    hot = hot_backward(start, span)
    turn = jnp.where(
        lax.broadcasted_iota(jnp.int32, (span, span), 0)
        + lax.broadcasted_iota(jnp.int32, (span, span), 1)
        == span - 1,
        1.0,
        0.0,
    ).astype(jnp.bfloat16)

    def attend(step, carry):
        r, g = step // 4, lax.rem(step, 4)
        cols = pl.ds(pl.multiple_of(g * 256, 256), 256)
        own_rows = pl.ds(pl.multiple_of(r * mine, local_len), mine)
        main_rows = pl.ds(pl.multiple_of(r * span, span), span)
        side_rows = pl.ds(pl.multiple_of(rows * span + r * 2 * local_len, local_len), 2 * local_len)
        above_tile = context_back[own_rows, cols]
        above = heads_in(above_tile)
        above_wide = above_tile.astype(jnp.float32)
        q_tile = query[own_rows, cols]
        zero = jnp.zeros((local_len, 256), jnp.float32)
        side_key = jnp.concatenate([zero, keys[side_rows, cols].astype(jnp.float32)], axis=0)
        side_value = jnp.concatenate([zero, values[side_rows, cols].astype(jnp.float32)], axis=0)
        spread = prob_own[own_rows, cols]
        grads = mm_back(above, values[main_rows, cols])
        own_grads = head_sums(above_wide * side_value)
        low, own_low = [], []
        for h in range(4):
            part = slice(h * mine, (h + 1) * mine)
            share = prob[step, part].astype(jnp.float32)
            own_share = spread[:, h * 64 : h * 64 + 1]
            weighted = share * grads[part]
            delta = jnp.sum(weighted, axis=1, keepdims=True) + own_share * own_grads[h]
            low.append((weighted - share * delta).astype(jnp.bfloat16))
            own_low.append(own_share * (own_grads[h] - delta))
        low = jnp.concatenate(low, axis=0)
        own_spread = head_lanes(own_low, 256)
        back = heads_out(mm(low, keys[main_rows, cols])) + own_spread * side_key
        query_back[own_rows, cols] = back.astype(jnp.bfloat16) * jnp.bfloat16(0.125)
        key_back[main_rows, cols] = mm_grad(low, heads_in(q_tile)).astype(jnp.bfloat16)
        value_back[main_rows, cols] = mm_grad(prob[step], above).astype(jnp.bfloat16)
        key_back[side_rows, cols] = (own_spread * q_tile.astype(jnp.float32))[local_len:].astype(
            jnp.bfloat16
        )
        value_back[side_rows, cols] = (spread * above_wide)[local_len:].astype(jnp.bfloat16)
        turned_low = skewed(mm(low, turn), local_len).astype(jnp.bfloat16)
        rel_total = heads_out(mm(turned_low, hot))
        near = lax.rem(lax.broadcasted_iota(jnp.int32, rel_total.shape, 1), BUCKETS) == 0
        rel_total = rel_total + jnp.where(near, head_lanes(own_low, 128), 0.0)
        rel_back[own_rows, pl.ds(pl.multiple_of(g * 128, 128), 128)] = rel_total.astype(
            jnp.bfloat16
        )
        return carry

    lax.fori_loop(0, 4 * rows, attend, 0)
    weight_ckey, weight_cvalue = fetch[w_ckey], fetch[w_cvalue]
    weight_query, weight_relative = fetch[w_query], fetch[w_relative]
    weight_key, weight_value = fetch[w_key], fetch[w_value]
    chips = rows * span // (rows * local_len)

    def states_body(cols):
        total = mm_back(ckey_back[...], weight_ckey[cols, :])
        total = total + mm_back(cvalue_back[...], weight_cvalue[cols, :])
        total = total.astype(jnp.bfloat16)
        for r in range(rows):
            for p in range(chips):
                at = r * span + p * local_len
                states_part[p, r, :, cols] = total[at : at + local_len]

    tiles(width, states_body)

    def hidden_body(cols):
        total = mm_back(key_back[...], weight_key[cols, :])
        total = total + mm_back(value_back[...], weight_value[cols, :])
        mains = total[: rows * span].astype(jnp.bfloat16)
        for r in range(rows):
            for p in range(chips):
                at = r * span + p * local_len
                main_part[p, r, :, cols] = mains[at : at + local_len]
        own = residual[:, cols] + mm_back(query_back[...], weight_query[cols, :])
        own = own + mm_back(rel_back[...], weight_relative[cols, :])
        for r in range(rows):
            for j in range(3):
                tile = own[r * mine + j * local_len : r * mine + (j + 1) * local_len]
                if j:
                    at = rows * span + (2 * r + j - 1) * local_len
                    tile = tile + total[at : at + local_len]
                hidden_own[j, r, :, cols] = tile

    tiles(width, hidden_body)


def finish_kernel(count, *refs):
    sums, (hidden_own, main_sum, states_sum) = refs[:count], refs[count : count + 3]
    outs, (hidden_grad, states_grad), sems = (
        refs[count + 3 : 2 * count + 3],
        refs[2 * count + 3 : 2 * count + 5],
        refs[2 * count + 5],
    )
    copies = [
        pltpu.make_async_copy(src, dst, sems.at[i])
        for i, (src, dst) in enumerate(zip(sums + (states_sum,), outs + (states_grad,)))
    ]
    for copy in copies:
        copy.start()
    hidden_grad[0] = hidden_own[0] + main_sum[...]
    hidden_grad[1:] = hidden_own[1:]
    for copy in copies:
        copy.wait()


def finish(sums, hidden_own, main_sum, states_sum):
    shapes = [jax.ShapeDtypeStruct(a.shape, a.dtype) for a in (*sums, hidden_own, states_sum)]
    place = [pl.BlockSpec(memory_space=pl.ANY)]
    vmem = [pl.BlockSpec(memory_space=pltpu.VMEM)]
    count = len(sums)
    return pl.pallas_call(
        lambda *refs: finish_kernel(count, *refs),
        out_shape=shapes,
        in_specs=vmem * (count + 3),
        out_specs=place * count + vmem + place,
        scratch_shapes=[pltpu.SemaphoreType.DMA((count + 1,))],
        compiler_params=pltpu.CompilerParams(vmem_limit_bytes=62 * 2**20),
        name="finish",
    )(*sums, hidden_own, main_sum, states_sum)


def plain_call(kernel, name, ins, spaces, outs, scratch, flops):
    space = {"v": pltpu.VMEM, "s": pltpu.SMEM, "a": pl.ANY}
    out_shape = [jax.ShapeDtypeStruct(shape, kind) for shape, kind in outs]
    moved = sum(a.size * a.dtype.itemsize for a in list(ins) + out_shape)
    return pl.pallas_call(
        kernel,
        out_shape=out_shape,
        in_specs=[pl.BlockSpec(memory_space=space[p]) for p in spaces],
        out_specs=[pl.BlockSpec(memory_space=pltpu.VMEM)] * len(outs),
        scratch_shapes=scratch,
        compiler_params=pltpu.CompilerParams(vmem_limit_bytes=62 * 2**20),
        cost_estimate=pl.CostEstimate(flops=flops, bytes_accessed=moved, transcendentals=0),
        name=name,
    )(*ins)


def copies_of(arrays):
    return [pltpu.VMEM(a.shape, a.dtype) for a in arrays] + [
        pltpu.SemaphoreType.DMA((len(arrays),))
    ]


def local(
    hidden,
    encoder,
    lengths,
    enc_lengths,
    w_query,
    w_key,
    w_value,
    w_attn_out,
    w_relative,
    w_cross_query,
    w_cross_key,
    w_cross_value,
    w_cross_out,
    w_up,
    w_down,
    gain_attn,
    gain_cross,
    gain_ffn,
    cotangent,
):
    ndp, chips = lax.axis_size("dp"), lax.axis_size("seq")
    devices = ndp * chips
    low, wide = jnp.bfloat16, jnp.float32
    _, rows, local_len, width = hidden.shape
    span, tokens = local_len * chips, 3 * rows * local_len
    weights = (
        w_key,
        w_value,
        w_query,
        w_relative,
        w_attn_out,
        w_cross_key,
        w_cross_value,
        w_cross_query,
        w_cross_out,
        w_up,
        w_down,
    )
    gains = jnp.stack([gain_attn, gain_cross, gain_ffn])
    kernels = chips == 4 and w_query.shape[0] % 128 == 0
    if kernels:
        gains = jnp.pad(gains, ((0, 13), (0, 0)))
        *whole, whole_gains, mains, states = gather_weights(
            weights + (gains,), hidden, encoder, ndp
        )
        whole = [w.reshape(-1, w.shape[-1]) for w in whole]
        whole_gains = whole_gains[:, :8]
    else:
        gains = jnp.pad(gains, ((0, 5), (0, 0)))
        whole = [lax.all_gather(w, "dp", axis=0, tiled=True) for w in weights]
        whole_gains = lax.all_gather(gains, "dp", axis=0)
        mains = lax.all_gather(hidden[0], "seq", axis=1)
        states = lax.all_gather(encoder, "seq", axis=1)
    mains, states = mains.reshape(-1, width), states.reshape(-1, width)
    gains = jnp.transpose(whole_gains.astype(wide), (1, 0, 2)).reshape(8, -1)
    (
        full_key,
        full_value,
        full_query,
        full_relative,
        full_attn_out,
        full_ckey,
        full_cvalue,
        full_cquery,
        full_cout,
        full_up,
        full_down,
    ) = whole
    ff = full_up.shape[1]
    every = rows * (span + 2 * local_len)
    fetched = (
        full_key,
        full_value,
        full_query,
        full_relative,
        full_ckey,
        full_cvalue,
        full_attn_out,
        full_cquery,
    )
    (
        hid,
        x_all,
        query,
        keys,
        values,
        prob,
        prob_own,
        context,
        ckeys,
        cvalues,
        normal,
        normal_scale,
        normed_low,
        cquery,
        cprob,
        ccontext,
    ) = plain_call(
        lambda *refs: forward_kernel(rows, local_len, *refs),
        "forward_attention",
        (hidden, mains, states, lengths, enc_lengths, gains) + fetched,
        "vvvssv" + "a" * len(fetched),
        [
            ((tokens, width), low),
            ((every, width), low),
            ((tokens, width), low),
            ((every, width), low),
            ((every, width), low),
            ((4 * rows, 12 * local_len, span), low),
            ((tokens, width), wide),
            ((tokens, width), low),
            ((rows * span, width), low),
            ((rows * span, width), low),
            ((tokens, width), wide),
            ((tokens, 128), wide),
            ((tokens, width), low),
            ((tokens, width), low),
            ((4 * rows, 12 * local_len, span), low),
            ((tokens, width), low),
        ],
        [
            pltpu.VMEM((tokens, full_relative.shape[1]), low),
            pltpu.VMEM((tokens, width), wide),
        ]
        + copies_of(fetched),
        12 * 10**9,
    )
    fetched = (full_cout, full_up, full_down)
    (
        output,
        crossed_low,
        activated,
        last_low,
        up_back,
        cross_grad,
        cross_low,
        ccontext_back,
        gain_middle,
    ) = plain_call(
        lambda *refs: middle_kernel(rows, local_len, *refs),
        "feed_forward",
        (normal, ccontext, gains, cotangent) + fetched,
        "vvvv" + "a" * len(fetched),
        [
            (hidden.shape, low),
            ((tokens, width), low),
            ((tokens, ff), low),
            ((tokens, width), low),
            ((tokens, ff), low),
            ((tokens, width), wide),
            ((tokens, width), low),
            ((tokens, width), low),
            ((3, 8, width), wide),
        ],
        [
            pltpu.VMEM((tokens, width), wide),
            pltpu.VMEM((tokens, 128), wide),
            pltpu.VMEM((tokens, ff), low),
            pltpu.VMEM((tokens, width), wide),
        ]
        + copies_of(fetched),
        14 * 10**9,
    )
    fetched = (
        full_cquery,
        full_attn_out,
        full_ckey,
        full_cvalue,
        full_query,
        full_relative,
        full_key,
        full_value,
    )
    (
        cquery_back,
        ckey_back,
        cvalue_back,
        attn_low,
        query_back,
        key_back,
        value_back,
        rel_back,
        hidden_own,
        main_part,
        states_part,
        gain_back,
    ) = plain_call(
        lambda *refs: backward_kernel(rows, local_len, *refs),
        "backward_attention",
        (
            ccontext_back,
            cross_grad,
            cquery,
            ckeys,
            cvalues,
            cprob,
            normal,
            normal_scale,
            gains,
            query,
            keys,
            values,
            prob,
            prob_own,
        )
        + fetched,
        "v" * 14 + "a" * len(fetched),
        [
            ((tokens, width), low),
            ((rows * span, width), low),
            ((rows * span, width), low),
            ((tokens, width), low),
            ((tokens, width), low),
            ((every, width), low),
            ((every, width), low),
            ((tokens, full_relative.shape[1]), low),
            (hidden.shape, wide),
            ((chips, rows, local_len, width), low),
            ((chips, rows, local_len, width), low),
            ((3, 8, width), wide),
        ],
        [pltpu.VMEM((tokens, width), wide), pltpu.VMEM((tokens, width), low)] + copies_of(fetched),
        14 * 10**9,
    )
    xs = [activated, crossed_low, ccontext, normed_low, context, hid, x_all, states]
    gs = [
        last_low,
        up_back,
        cross_low,
        cquery_back,
        attn_low,
        query_back,
        rel_back,
        key_back,
        value_back,
        ckey_back,
        cvalue_back,
    ]
    pairs = [(0, 0), (1, 1), (2, 2), (3, 3), (4, 4), (5, 5), (5, 6), (6, 7), (6, 8), (7, 9), (7, 10)]
    gain_parts = jnp.sum(gain_middle + gain_back, axis=1)
    if kernels:
        gain_parts = jnp.transpose(gain_parts.reshape(3, devices, -1), (1, 0, 2))
        gain_parts = jnp.pad(gain_parts, ((0, 0), (0, 5), (0, 128 - gain_parts.shape[2])))
        gain_parts = gain_parts.reshape(2, 2, ndp // 2, 2, 8, 128)
        shares = (main_part, states_part)
        shares = [a.reshape((2, 2) + a.shape[1:]) for a in shares]
        *sums, gain_sums, main_sum, states_sum = reduce_grads(
            xs, gs, pairs, gain_parts, shares, ndp // 2
        )
        gain_sums = gain_sums[:3, : width // devices]
        *sums, hidden_grad, states_sum = finish(sums, hidden_own, main_sum, states_sum)
    else:
        sums = [
            lax.psum_scatter(
                weight_grad(xs[i], gs[j]), ("seq", "dp"), scatter_dimension=0, tiled=True
            )
            for i, j in pairs
        ]
        gain_sums = lax.psum_scatter(gain_parts, ("seq", "dp"), scatter_dimension=1, tiled=True)
        main_sum, states_sum = (
            lax.psum_scatter(part, "seq", scatter_dimension=0).astype(wide)
            for part in (main_part, states_part)
        )
        hidden_grad = hidden_own.at[0].add(main_sum)
    gainattn_sum, gaincross_sum, gainffn_sum = gain_sums
    (
        down_sum,
        up_sum,
        cout_sum,
        cquery_sum,
        outproj_sum,
        query_sum,
        relative_sum,
        keyw_sum,
        valuew_sum,
        ckey_sum,
        cvalue_sum,
    ) = sums
    return (
        output,
        hidden_grad,
        states_sum,
        query_sum,
        keyw_sum,
        valuew_sum,
        outproj_sum,
        relative_sum,
        cquery_sum,
        ckey_sum,
        cvalue_sum,
        cout_sum,
        up_sum,
        down_sum,
        gainattn_sum,
        gaincross_sum,
        gainffn_sum,
    )


def solution(mesh):
    in_specs = (
        P(None, "dp", "seq", None),
        P("dp", "seq", None),
        P("dp"),
        P("dp"),
        P("dp", None),
        P("dp", None),
        P("dp", None),
        P("dp", None),
        P("dp", None),
        P("dp", None),
        P("dp", None),
        P("dp", None),
        P("dp", None),
        P("dp", None),
        P("dp", None),
        P("dp"),
        P("dp"),
        P("dp"),
        P(None, "dp", "seq", None),
    )
    out_specs = (
        P(None, "dp", "seq", None),
        P(None, "dp", "seq", None),
        P("dp", "seq", None),
        P(("seq", "dp"), None),
        P(("seq", "dp"), None),
        P(("seq", "dp"), None),
        P(("seq", "dp"), None),
        P(("seq", "dp"), None),
        P(("seq", "dp"), None),
        P(("seq", "dp"), None),
        P(("seq", "dp"), None),
        P(("seq", "dp"), None),
        P(("seq", "dp"), None),
        P(("seq", "dp"), None),
        P(("seq", "dp")),
        P(("seq", "dp")),
        P(("seq", "dp")),
    )
    return jax.shard_map(local, mesh=mesh, in_specs=in_specs, out_specs=out_specs, check_vma=False)
```

time: 760 us -> 472 us (0.62)
  local copies, waits for them, and re-layouts: 182 us -> 2.11 us
  matrix products: 147 us -> 0 us
  Pallas kernels: 319 us -> 459 us
  other arithmetic: 80 us -> 3.56 us
  between operations: 15.6 us -> 0.95 us
    dot_general x36 -> x0, matrix products: 147 us -> none  [the longest x11 45.8 us: project_back(): jnp.einsum('ne,de->nd', flatten_rows(grad_rows), weight, preferred_elemen...]
    pallas_call x0 -> x4, Pallas kernels: none -> 127 us  [the longest x3 122 us: plain_call(): pl.pallas_call(kernel, out_shape=out_shape, in_specs=[pl.BlockSpec(memory...]
    unnamed x206 -> x3, local copies, waits for them, and re-layouts: 66.4 us -> 0.04 us
    convert_element_type x19 -> x0, local copies, waits for them, and re-layouts: 42 us -> none  [the longest x3 10.1 us: local(): cross_context_low = cross_context.reshape(flat_shape).astype(jnp.bfloat16)]
    reduce_sum x13 -> x1, other arithmetic: 32.8 us -> 0.93 us  [local(): gain_parts = jnp.sum(gain_middle + gain_back, axis=1)]
    convert_element_type x12 -> x0, other arithmetic: 29.1 us -> none  [the longest x1 15.2 us: local(): activated_low = activated.astype(jnp.bfloat16)]
    reshape x6 -> x1, local copies, waits for them, and re-layouts: 19.8 us -> 0.09 us  [local(): gain_parts = jnp.transpose(gain_parts.reshape(3, devices, -1), (1, 0, 2))]
    pallas_call x1, Pallas kernels: 173 us -> 186 us  [reduce_grads(): pl.pallas_call(lambda *refs: reduce_grads_kernel(plan, nz, len(xs), len(g...]
  transfers between devices with their start and end apart: 8 -> 0, of which waited for: 1 -> 0; matrix products, arithmetic and copies ran while one was open for 33% -> 0% of each run, Pallas kernels for 0% -> 0%
where the time goes in v2:
time: 472 us; the launch traced here: 466 us
  Pallas kernels  459 us (97%)
    pallas_call x1, Pallas kernels, reduce_grads(): pl.pallas_call(lambda *refs: reduce_grads_kernel(plan, nz, len(xs), len(g...  186 us
    pallas_call x1, Pallas kernels, gather_weights(): pl.pallas_call(lambda *refs: gather_weights_kernel(count, nz, *refs), out...  146 us
    pallas_call x3, Pallas kernels, plain_call(): pl.pallas_call(kernel, out_shape=out_shape, in_specs=[pl.BlockSpec(memory...  122 us

profile of v2, /device:TPU:0, one launch (start us, length us, event | category | flops | bytes accessed | tf_op | source)
XLA Modules:
  0.0 465.5 jit_solution(8425504954584240015)
XLA Ops:
  0.7 1.3 fusion.4.refs_11_
  1.9 146.0 %gather_weights.1 = (bf16[8,128,1024]{2,1,0:T(8,128)(2,1)}, bf16[8,128,1024]{2,1,0:T(8,128)(2,1)}, bf16[8,128,1024]{2,1,0:T(8,128)(2,1)}, bf16[8,128,512]{2,1,0:...) custom-call(bf16[128,1024]{1,0:T(8,128)(2,1)} %refs_0_.2, ...), custom_call_target="tpu_custom_call" | custom-call | tf_op jit(solution)/shard_map/gather_weights/pallas_call | solution.py:226
  147.9 1.3 convert_bitcast_fusion.refs_5_.refs_2_.refs_8_
  149.3 42.0 %forward_attention.1 = (bf16[384,1024]{1,0:T(8,128)(2,1)}, bf16[768,1024]{1,0:T(8,128)(2,1)}, bf16[384,1024]{1,0:T(8,128)(2,1)}, bf16[768,1024]{1,0:T(8,128)(2,1...) custom-call(bf16[3,2,64,1024]{3,2,1,0:T(8,128)(2,1)} %refs_0_.3, ...), custom_call_target="tpu_custom_call" | custom-call | flops 12000000000 | bytes 39813136 | tf_op jit(solution)/shard_map/forward_attention/pallas_call | solution.py:1022
  191.3 36.4 %feed_forward.1 = (bf16[3,2,64,1024]{3,2,1,0:T(8,128)(2,1)}, bf16[384,1024]{1,0:T(8,128)(2,1)}, bf16[384,4096]{1,0:T(8,128)(2,1)}, bf16[384,1024]{1,0:T(8,128)(2...) custom-call(f32[384,1024]{1,0:T(8,128)} %get-tuple-element.106.refs_, ...), custom_call_target="tpu_custom_call" | custom-call | flops 14000000000 | bytes 33947648 | tf_op jit(solution)/shard_map/feed_forward/pallas_call | solution.py:1022
  227.7 0.0 copy-start
  227.7 43.5 %backward_attention.1 = (bf16[384,1024]{1,0:T(8,128)(2,1)}, bf16[512,1024]{1,0:T(8,128)(2,1)}, bf16[512,1024]{1,0:T(8,128)(2,1)}, bf16[384,1024]{1,0:T(8,128)(2,...) custom-call(bf16[384,1024]{1,0:T(8,128)(2,1)} %get-tuple-element.121, ...), custom_call_target="tpu_custom_call" | custom-call | flops 14000000000 | bytes 46333952 | tf_op jit(solution)/shard_map/backward_attention/pallas_call | solution.py:1022
  271.2 0.0 copy-done
  271.2 0.9 add_reduce_fusion
  272.1 0.1 reshape.105
  272.2 0.7 pad.9.clone
  272.9 186.0 %reduce_grads.1 = (f32[128,1024]{1,0:T(8,128)}, f32[32,4096]{1,0:T(8,128)}, f32[32,1024]{1,0:T(8,128)}, f32[32,1024]{1,0:T(8,128)}, f32[32,1024]{1,0:T(8,128)}, ...) custom-call(bf16[384,4096]{1,0:T(8,128)(2,1)} %get-tuple-element.112, ...), custom_call_target="tpu_custom_call" | custom-call | tf_op jit(solution)/shard_map/reduce_grads/pallas_call | solution.py:433
  458.9 5.1 %finish.1 = (f32[128,1024]{1,0:T(8,128)}, f32[32,4096]{1,0:T(8,128)}, f32[32,1024]{1,0:T(8,128)}, f32[32,1024]{1,0:T(8,128)}, f32[32,1024]{1,0:T(8,128)}, /*inde...) custom-call(f32[128,1024]{1,0:T(8,128)} %get-tuple-element.145.refs_, ...), custom_call_target="tpu_custom_call" | custom-call | tf_op jit(solution)/shard_map/finish/pallas_call | solution.py:1007
  464.0 1.3 slice_bitcast_fusion
  (1 shorter events, 0.0 us)
Async XLA Ops:
  227.7 43.5 %copy-start = (f32[3,8,1024]{2,1,0:T(8,128)S(1)}, f32[3,8,1024]{2,1,0:T(8,128)}, u32[]{:S(2)}) copy-start(f32[3,8,1024]{2,1,0:T(8,128)} %get-tuple-element.141) | copy-start | bytes 294916
